TPU v7x, 128 devices: a whole 4x4x4 slice. The times are simulated.
128 devices in a mesh: dp: 16 (over x, y_hi, core), tensor: 8 (over z, y_lo).
Axes of the slice: x: 4, y: 4 (y_hi: 2, y_lo: 2; y = y_hi * 2 + y_lo), z: 4, core: 2. Of those that a mesh axis runs over, the one named last changes fastest.
Arguments:
- tokens: bfloat16 [16, 2, 512, 2048], P('dp', None, 'tensor'), may hold values from -6 to 6
- lengths: int32 [16, 2], P('dp'), may hold values from 128 to 512, as said below
- cotangent: bfloat16 [16, 2, 512, 2048], P('dp', None, 'tensor'), may hold values from -6 to 6
- attn_gain: float32 [2048], replicated, may hold values from 0.1 to 1.9
- mixer_in: bfloat16 [2048, 4, 2048], P(None, None, 'tensor'), may hold values from -0.125 to 0.125
- rate_proj: bfloat16 [2048, 2, 16], P(None, None, 'tensor'), may hold values from -0.125 to 0.125
- conv_weight: float32 [3, 4, 2048], P(None, None, 'tensor'), may hold values from -2.5 to 2.5
- decay_rate: float32 [16], P('tensor'), may hold values from 0.05 to 4
- decay_bias: float32 [16], P('tensor'), may hold values from -5 to -2
- out_gain: float32 [128], replicated, may hold values from 0.25 to 1.75
- out_proj: bfloat16 [2048, 2048], P('tensor'), may hold values from -0.25 to 0.25
- ffn_gain: float32 [2048], replicated, may hold values from 0.1 to 1.9
- gate_up: bfloat16 [2048, 2, 5632], P(None, None, 'tensor'), may hold values from -0.125 to 0.125
- down_proj: bfloat16 [5632, 2048], P('tensor'), may hold values from -0.109375 to 0.109375
Outputs:
- layer_out: bfloat16 [16, 2, 512, 2048], P('dp', None, 'tensor')
- d_tokens: bfloat16 [16, 2, 512, 2048], P('dp', None, 'tensor')
- d_attn_gain: float32 [2048], replicated
- d_mixer_in: float32 [2048, 4, 2048], P(None, None, 'tensor')
- d_rate_proj: float32 [2048, 2, 16], P(None, None, 'tensor')
- d_conv_weight: float32 [3, 4, 2048], P(None, None, 'tensor')
- d_decay_rate: float32 [16], P('tensor')
- d_decay_bias: float32 [16], P('tensor')
- d_out_gain: float32 [128], replicated
- d_out_proj: float32 [2048, 2048], P('tensor')
- d_ffn_gain: float32 [2048], replicated
- d_gate_up: float32 [2048, 2, 5632], P(None, None, 'tensor')
- d_down_proj: float32 [5632, 2048], P('tensor')
Inputs may be any that keep to these rules, and one draw needn't show every extreme that they name: `lengths`: in each group at least one microbatch has all 512 tokens live; positions at or past a microbatch's length are padding.
All inputs are finite; a program needn't handle non-finite values.
Results may differ from a plain program's by a relative error of at most 0.04.
Values may be sent and summed in bfloat16 or wider, within the bound.
No kernel may reach another device: no remote copies, remote signals or barrier semaphores. Data moves between devices by JAX's collectives and lax.ppermute only.
A program may use at most 320 MiB of HBM per device.

v0:
```python
import jax, jax.numpy as jnp
from jax import lax
from jax.experimental import pallas as pl
from jax.experimental.pallas import tpu as pltpu
from jax.sharding import Mesh, PartitionSpec as P

EPS = 1e-06
BLOCK = 64
HS = 128
HEADS = 2
WIDTH = HEADS * HS
F32 = jnp.float32
HIGHEST = lax.Precision.HIGHEST
HIGH = lax.Precision.HIGH
LOW = lax.Precision.DEFAULT
P_INV = HIGH
P_ST = HIGH
P_GR = HIGH
P_BST = LOW
P_BGR = LOW


def dot2(a, b, ca, cb, precision):
    return lax.dot_general(a, b, (((ca,), (cb,)), ((), ())), precision=precision, preferred_element_type=F32)


def bdot(a, b, ca, cb, precision):
    if precision == LOW:
        a, b = a.astype(jnp.bfloat16), b.astype(jnp.bfloat16)
    return jnp.stack([dot2(a[i], b[i], ca, cb, precision) for i in range(a.shape[0])])


def split_heads(rows):
    blocks = rows.shape[0] // BLOCK
    return jnp.concatenate(
        [rows[:, h * HS : (h + 1) * HS].reshape(blocks, BLOCK, HS) for h in range(HEADS)], axis=0
    )


def join_heads(stacked):
    blocks = stacked.shape[0] // HEADS
    return jnp.concatenate(
        [stacked[h * blocks : (h + 1) * blocks].reshape(blocks * BLOCK, HS) for h in range(HEADS)], axis=1
    )


def shift_down(rows, steps):
    if steps == 0:
        return rows
    place = lax.broadcasted_iota(jnp.int32, rows.shape, 0)
    return jnp.where(place >= steps, pltpu.roll(rows, steps, 0), 0.0)


def shift_up(rows, steps):
    if steps == 0:
        return rows
    size = rows.shape[0]
    place = lax.broadcasted_iota(jnp.int32, rows.shape, 0)
    return jnp.where(place < size - steps, pltpu.roll(rows, size - steps, 0), 0.0)


def sigmoid(v):
    return 1.0 / (1.0 + jnp.exp(-v))


def softplus(v):
    return jnp.maximum(v, 0.0) + jnp.log1p(jnp.exp(-jnp.abs(v)))


def convolve(rows, taps):
    out = rows * taps[3:4, :]
    for j in range(3):
        out = out + shift_down(rows, 3 - j) * taps[j : j + 1, :]
    return out


def columns(table, blocks, first):
    return jnp.concatenate(
        [table[:, first + h : first + h + 1].reshape(blocks, BLOCK, 1) for h in range(HEADS)], axis=0
    )


def rows_of(turned, first):
    return jnp.concatenate([turned[:, first + h : first + h + 1, :] for h in range(HEADS)], axis=0)


def gates(rates, decay_rate, decay_bias):
    blocks = rates.shape[0] // BLOCK
    soft = softplus(rates + decay_bias)
    logdecay = (-decay_rate * soft).reshape(blocks, BLOCK, 128)
    row = lax.broadcasted_iota(jnp.int32, (BLOCK, BLOCK), 0)
    col = lax.broadcasted_iota(jnp.int32, (BLOCK, BLOCK), 1)
    ones = (row >= col).astype(F32)
    cumul = jnp.stack([dot2(ones, logdecay[n], 1, 0, HIGHEST) for n in range(blocks)])
    update = sigmoid(rates).reshape(blocks, BLOCK, 128)
    lane = lax.broadcasted_iota(jnp.int32, (blocks, BLOCK, 128), 2)
    table = jnp.where(lane < 2, cumul, update)
    turned = jnp.stack([jnp.transpose(table[n], (1, 0)) for n in range(blocks)])
    flat = table.reshape(blocks * BLOCK, 128)
    return soft, columns(flat, blocks, 0), rows_of(turned, 0), columns(flat, blocks, 2), rows_of(turned, 2)


def activate(rows, taps):
    pre = convolve(rows, taps)
    sig = sigmoid(pre)
    return pre, sig, pre * sig


def lower_inverse(strict):
    row = lax.broadcasted_iota(jnp.int32, strict.shape, 1)
    col = lax.broadcasted_iota(jnp.int32, strict.shape, 2)
    size = 1
    inverse = jnp.where(row == col, 1.0, 0.0)
    while size < BLOCK:
        lower = jnp.where((row // (2 * size) == col // (2 * size)) & (row // size != col // size), strict, 0.0)
        if size == 1:
            inverse = inverse - lower
        else:
            inverse = inverse - bdot(inverse, bdot(lower, inverse, 2 - 1, 0, P_INV), 1, 0, P_INV)
        size *= 2
    return inverse


def parts(queries, keys, cum_c, cum_r, upd_r, precision):
    shape = (queries.shape[0], BLOCK, BLOCK)
    row = lax.broadcasted_iota(jnp.int32, shape, 1)
    col = lax.broadcasted_iota(jnp.int32, shape, 2)
    both = bdot(jnp.concatenate([keys, queries], axis=1), keys, 1, 1, precision)
    ratio = jnp.where(row >= col, jnp.exp(jnp.where(row >= col, cum_c - cum_r, 0.0)), 0.0)
    scaled = ratio * upd_r
    return row, col, scaled, ratio, both[:, :BLOCK], both[:, BLOCK:]


def unit(v):
    return lax.rsqrt(jnp.sum(v * v, -1, keepdims=True) + EPS)


def place(slots, n):
    first = (slots[n] * pl.num_programs(0) + pl.program_id(0)) * BLOCK
    return pl.ds(pl.multiple_of(first, BLOCK), BLOCK)


def in_order(slots, pieces, held, target):
    @pl.when(pl.program_id(0) == 0)
    def _():
        first = 0
        for piece in pieces:
            held[first : first + piece.shape[0], :] = piece[...]
            first += piece.shape[0]

    for n in range(target.shape[0] // BLOCK):
        target[n * BLOCK : (n + 1) * BLOCK, :] = held[place(slots, n), :]


def out_slots(held, outs):
    @pl.when(pl.program_id(0) == pl.num_programs(0) - 1)
    def _():
        size = outs[0].shape[0]
        for i, out in enumerate(outs):
            out[...] = held[i * size : (i + 1) * size, :]


def fwd_kernel(slots, *refs):
    pieces, refs = refs[:9], refs[9:]
    w_ref, conv_ref, dec_ref, gain_ref, out_w_ref, *sums, normed_ref, proj_ref, rows_ref = refs[:16]
    out_ref, err_ref, inv_ref, sk_ref, state_ref, step_ref, held_ref = refs[16:]
    width = WIDTH
    in_order(slots, pieces, held_ref, normed_ref)
    proj_ref[...] = dot2(normed_ref[...], w_ref[...], 1, 0, None)
    _, _, act_q = activate(proj_ref[:, 0:width], conv_ref[0])
    _, _, act_k = activate(proj_ref[:, width : 2 * width], conv_ref[1])
    _, _, act_v = activate(proj_ref[:, 2 * width : 3 * width], conv_ref[2])
    act_q, act_k, values = split_heads(act_q), split_heads(act_k), split_heads(act_v)
    queries = act_q * (unit(act_q) * HS**-0.5)
    keys = act_k * unit(act_k)
    _, cum_c, cum_r, upd_c, upd_r = gates(proj_ref[:, 4 * width :], dec_ref[0:1, :], dec_ref[1:2, :])
    row, col, scaled, _, kk, qk = parts(queries, keys, cum_c, cum_r, upd_r, P_GR)
    inverse = lower_inverse(jnp.where(row > col, scaled * kk, 0.0))
    inv_ref[...] = inverse
    attend = scaled * qk
    grow = jnp.exp(cum_c)
    last = cum_c[:, BLOCK - 1 :, :]
    tail = keys * (jnp.exp(last - cum_c) * upd_c)
    solved = bdot(inverse, jnp.concatenate([values, grow * keys], axis=2), 1, 0, P_ST)
    sk_ref[...] = solved[:, :, HS:]
    carried = bdot(tail, solved, 0, 0, P_ST)
    n = carried.shape[0]
    row2 = lax.broadcasted_iota(jnp.int32, (n, HS, HS), 1)
    col2 = lax.broadcasted_iota(jnp.int32, (n, HS, HS), 2)
    step = jnp.where(row2 == col2, jnp.exp(last), 0.0) - carried[:, :, HS:]
    step_ref[...] = step
    blocks = n // HEADS
    states = []
    for h in range(HEADS):
        state = jnp.zeros((HS, HS), F32)
        states.append(state)
        for i in range(blocks - 1):
            at = h * blocks + i
            state = carried[at, :, :HS] + (dot2(step[at], state, 1, 0, P_ST) if i else 0.0)
            states.append(state)
    states = jnp.stack(states)
    state_ref[...] = states
    seen = bdot(jnp.concatenate([solved[:, :, HS:], grow * queries], axis=1), states, 1, 0, P_ST)
    errors = solved[:, :, :HS] - seen[:, :BLOCK]
    err_ref[...] = errors
    outputs = seen[:, BLOCK:] + bdot(attend, errors, 1, 0, P_ST)
    out_ref[...] = outputs
    scale = lax.rsqrt(jnp.mean(outputs * outputs, -1, keepdims=True) + EPS)
    gate = proj_ref[:, 3 * width : 4 * width]
    rows = (join_heads(outputs * scale * gain_ref[...]) * (gate * sigmoid(gate))).astype(jnp.bfloat16)
    rows_ref[...] = rows
    product = dot2(rows, out_w_ref[...], 1, 0, None).astype(jnp.bfloat16)
    for n in range(blocks):
        held_ref[place(slots, n), :] = product[n * BLOCK : (n + 1) * BLOCK]
    out_slots(held_ref, sums)


def unit_back(act, d_norm, factor):
    r = unit(act)
    return factor * (r * d_norm - act * (r * r * r) * jnp.sum(d_norm * act, -1, keepdims=True))


def bwd_kernel(slots, *refs):
    pieces, refs = refs[:9], refs[9:]
    proj_ref, conv_ref, dec_ref, gain_ref, out_w_ref, out_ref, err_ref, inv_ref, sk_ref, state_ref, step_ref = refs[:11]
    grad_ref, dproj_ref, dconv_ref, dsmall_ref, held_ref = refs[11:]
    width = WIDTH
    in_order(slots, pieces, held_ref, grad_ref)
    d_rows = dot2(grad_ref[...], out_w_ref[...], 1, 1, None)
    n = err_ref.shape[0]
    blocks = n // HEADS
    rates = proj_ref[:, 4 * width :]
    pre_q, sig_q, full_q = activate(proj_ref[:, 0:width], conv_ref[0])
    pre_k, sig_k, full_k = activate(proj_ref[:, width : 2 * width], conv_ref[1])
    act_q, act_k = split_heads(full_q), split_heads(full_k)
    queries = act_q * (unit(act_q) * HS**-0.5)
    keys = act_k * unit(act_k)
    soft, cum_c, cum_r, upd_c, upd_r = gates(rates, dec_ref[0:1, :], dec_ref[1:2, :])
    row, col, scaled, ratio, kk, qk = parts(queries, keys, cum_c, cum_r, upd_r, P_BGR)
    attend = scaled * qk
    grow = jnp.exp(cum_c)
    last = cum_c[:, BLOCK - 1 :, :]
    fade = jnp.exp(last - cum_c)
    weight = fade * upd_c
    tail = keys * weight
    outputs, errors, states = out_ref[...], err_ref[...], state_ref[...]

    gate = proj_ref[:, 3 * width : 4 * width]
    sig_g = sigmoid(gate)
    scale = lax.rsqrt(jnp.mean(outputs * outputs, -1, keepdims=True) + EPS)
    gain = gain_ref[...]
    normal = outputs * scale
    d_gained = split_heads(d_rows * (gate * sig_g))
    d_gate = d_rows * join_heads(normal * gain) * (sig_g * (1.0 + gate * (1.0 - sig_g)))
    dproj_ref[:, 3 * width : 4 * width] = d_gate.astype(jnp.bfloat16)
    d_gain = jnp.sum((d_gained * normal).reshape(n * BLOCK, HS), 0, keepdims=True)
    d_normal = d_gained * gain
    d_out = scale * d_normal - outputs * (scale * scale * scale) * jnp.mean(d_normal * outputs, -1, keepdims=True)

    d_err_own = bdot(attend, d_out, 0, 0, P_BST)
    to_state = bdot(
        jnp.concatenate([grow * queries, -sk_ref[...]], axis=1),
        jnp.concatenate([d_out, d_err_own], axis=1), 0, 0, P_BST,
    )
    d_ends = [None] * n
    for h in range(HEADS):
        d_end = jnp.zeros((HS, HS), F32)
        for i in range(blocks - 1, -1, -1):
            at = h * blocks + i
            d_ends[at] = d_end
            if i:
                d_end = to_state[at] + (dot2(step_ref[at], d_end, 0, 0, P_BST) if i < blocks - 1 else 0.0)
    d_ends = jnp.stack(d_ends)
    d_err = d_err_own + bdot(tail, d_ends, 1, 0, P_BST)
    d_val = bdot(inv_ref[...], d_err, 0, 0, P_BST)
    pair = jnp.concatenate([d_out, d_val], axis=1)
    by_err = bdot(pair, errors, 1, 1, P_BGR)
    by_state = bdot(pair, states, 1, 1, P_BGR)
    d_tail = bdot(errors, d_ends, 1, 1, P_BGR)
    raw_attend = jnp.where(row >= col, by_err[:, :BLOCK], 0.0)
    raw_system = jnp.where(row > col, -by_err[:, BLOCK:], 0.0)
    d_qk = raw_attend * scaled
    d_kk = raw_system * scaled
    d_seen_q, d_seen_k = by_state[:, :BLOCK], -by_state[:, BLOCK:]
    stacked = jnp.concatenate([d_qk, d_kk], axis=1)
    from_left = bdot(stacked, keys, 1, 0, P_BGR)
    from_right = bdot(stacked, jnp.concatenate([queries, keys], axis=1), 0, 0, P_BGR)
    d_queries = grow * d_seen_q + from_left[:, :BLOCK]
    d_keys = grow * d_seen_k + weight * d_tail + from_left[:, BLOCK:] + from_right

    mixed = ratio * (raw_attend * qk + raw_system * kk)
    moved = mixed * upd_r
    eye = row == col
    over_upd = jnp.sum(mixed, 1, keepdims=True)
    tail_dot = jnp.sum(keys * d_tail, -1, keepdims=True)
    tail_part = weight * tail_dot
    d_upd = jnp.sum(jnp.where(eye, over_upd, 0.0), -1, keepdims=True) + fade * tail_dot
    d_cum = jnp.sum(moved - jnp.where(eye, over_upd * upd_r, 0.0), -1, keepdims=True)
    d_cum = d_cum + grow * jnp.sum(d_seen_q * queries + d_seen_k * keys, -1, keepdims=True) - tail_part
    d_last = jnp.sum(tail_part, 1, keepdims=True) + jnp.exp(last) * jnp.sum(
        jnp.sum(states * d_ends, 1, keepdims=True), 2, keepdims=True
    )
    ones = (lax.broadcasted_iota(jnp.int32, (BLOCK, BLOCK), 0) <= lax.broadcasted_iota(jnp.int32, (BLOCK, BLOCK), 1)).astype(F32)
    lane = lax.broadcasted_iota(jnp.int32, (blocks, BLOCK, 128), 2)
    spread = jnp.where(lane == 0, d_cum[:blocks], jnp.where(lane == 1, d_cum[blocks:], 0.0))
    d_log = jnp.stack([dot2(ones, spread[i], 1, 0, HIGHEST) for i in range(blocks)])
    d_log = d_log + jnp.where(lane == 0, d_last[:blocks], jnp.where(lane == 1, d_last[blocks:], 0.0))
    d_update = jnp.where(lane == 2, d_upd[:blocks], jnp.where(lane == 3, d_upd[blocks:], 0.0))
    d_log = d_log.reshape(blocks * BLOCK, 128)
    d_update = d_update.reshape(blocks * BLOCK, 128)
    update = sigmoid(rates)
    decay_rate, decay_bias = dec_ref[0:1, :], dec_ref[1:2, :]
    d_first = d_log * -decay_rate * sigmoid(rates + decay_bias)
    d_rates = (d_first + d_update * update * (1.0 - update)).astype(jnp.bfloat16)
    dproj_ref[:, 4 * width :] = d_rates
    small = jnp.concatenate(
        [
            jnp.sum(d_log * -soft, 0, keepdims=True),
            jnp.sum(d_first, 0, keepdims=True),
            d_gain,
            jnp.zeros((5, 128), F32),
        ],
        axis=0,
    )
    dsmall_ref[...] = small

    for c, (pre, sig, d_act) in enumerate(
        (
            (pre_q, sig_q, join_heads(unit_back(act_q, d_queries, HS**-0.5))),
            (pre_k, sig_k, join_heads(unit_back(act_k, d_keys, 1.0))),
            (None, None, join_heads(d_val)),
        )
    ):
        rows = proj_ref[:, c * width : (c + 1) * width]
        taps = conv_ref[c]
        if pre is None:
            pre, sig, _ = activate(rows, taps)
        d_pre = d_act * (sig * (1.0 + pre * (1.0 - sig)))
        d_in = d_pre * taps[3:4, :]
        sums = []
        for j in range(3):
            d_in = d_in + shift_up(d_pre, 3 - j) * taps[j : j + 1, :]
            sums.append(jnp.sum(d_pre * shift_down(rows, 3 - j), 0, keepdims=True))
        sums.append(jnp.sum(d_pre * rows, 0, keepdims=True))
        dproj_ref[:, c * width : (c + 1) * width] = d_in.astype(jnp.bfloat16)
        dconv_ref[c] = jnp.concatenate(sums, axis=0)


def whole(shape):
    return pl.BlockSpec(tuple(shape), lambda i, slots: (0,) * len(shape), pipeline_mode=pl.Buffered(1))


def each(shape):
    return pl.BlockSpec((None,) + tuple(shape[1:]), lambda i, slots: (i,) + (0,) * (len(shape) - 1))


def kernel_call(kernel, name, micros, outs, ins, held, time):
    slots, rest = ins[0], ins[1:]
    spec = lambda a: each(a.shape) if len(a.shape) > 2 and a.shape[0] == micros else whole(a.shape)
    return pl.pallas_call(
        kernel,
        grid_spec=pltpu.PrefetchScalarGridSpec(
            num_scalar_prefetch=1,
            grid=(micros,),
            in_specs=[spec(a) for a in rest],
            out_specs=[spec(o) for o in outs],
            scratch_shapes=[pltpu.VMEM(held, jnp.bfloat16)],
        ),
        out_shape=outs,
        compiler_params=pltpu.CompilerParams(vmem_limit_bytes=62 * 2**20),
        cost_estimate=cost(time),
        name=name,
    )(slots, *rest)


def mixer_fwd(slots, pieces, w_in, conv, dec, gain, out_proj, micros):
    rows, features = 8 * pieces[0].shape[0], pieces[0].shape[1]
    own = rows // micros
    n = HEADS * own // BLOCK
    low = lambda *shape: jax.ShapeDtypeStruct(shape, jnp.bfloat16)
    wide = lambda *shape: jax.ShapeDtypeStruct((micros,) + shape, F32)
    outs = [low(rows // 8, features)] * 8
    outs += [low(micros, own, features), wide(own, w_in.shape[1]), low(micros, own, WIDTH)]
    outs += [wide(n, BLOCK, HS), wide(n, BLOCK, HS), wide(n, BLOCK, BLOCK), wide(n, BLOCK, HS)]
    outs += [wide(n, HS, HS), wide(n, HS, HS)]
    ins = (slots, *pieces, w_in, conv, dec, gain, out_proj)
    done = kernel_call(fwd_kernel, "mixer_fwd", micros, outs, ins, (rows, features), 30)
    return done[:8], done[8:11], done[11:]


def mixer_bwd(slots, pieces, mixed, conv, dec, gain, out_proj, saved, micros):
    rows, features = 8 * pieces[0].shape[0], pieces[0].shape[1]
    outs = [
        jax.ShapeDtypeStruct((micros, rows // micros, features), jnp.bfloat16),
        jax.ShapeDtypeStruct(mixed.shape, jnp.bfloat16),
        jax.ShapeDtypeStruct((micros,) + conv.shape, F32),
        jax.ShapeDtypeStruct((micros, 8, 128), F32),
    ]
    ins = (slots, *pieces, mixed, conv, dec, gain, out_proj, *saved)
    return kernel_call(bwd_kernel, "mixer_bwd", micros, outs, ins, (rows, features), 32)


def normed_kernel(slots, d_ref, w_ref, *refs):
    outs, held = refs[:-1], refs[-1]
    micros, blocks, size, _ = d_ref.shape

    @pl.when(pl.program_id(0) == 0)
    def _():
        for n in range(blocks):
            for m in range(micros):
                first = pl.multiple_of((slots[n] * micros + m) * size, size)
                held[pl.ds(first, size), :] = d_ref[m, n]

    product = dot2(held[...], w_ref[...], 1, 1, None).astype(jnp.bfloat16)
    for i, out in enumerate(outs):
        out[...] = product[i * size * micros : (i + 1) * size * micros]


def normed_grad(slots, d_mixed, w_in):
    micros, own, width = d_mixed.shape
    features = w_in.shape[0]
    slot = jax.ShapeDtypeStruct((micros * own // 8, features), jnp.bfloat16)
    shape = (micros, 8, own // 8, width)
    steps = 4
    return pl.pallas_call(
        normed_kernel,
        grid_spec=pltpu.PrefetchScalarGridSpec(
            num_scalar_prefetch=1,
            grid=(steps,),
            in_specs=[
                pl.BlockSpec(shape, lambda i, slots: (0, 0, 0, 0)),
                pl.BlockSpec((features // steps, width), lambda i, slots: (i, 0)),
            ],
            out_specs=[pl.BlockSpec((slot.shape[0], features // steps), lambda i, slots: (0, i))] * 8,
            scratch_shapes=[pltpu.VMEM((micros * own, width), jnp.bfloat16)],
        ),
        out_shape=[slot] * 8,
        compiler_params=pltpu.CompilerParams(vmem_limit_bytes=48 * 2**20),
        cost_estimate=cost(8),
        name="normed_grad",
    )(slots, d_mixed.reshape(shape), w_in)


UP = [(i, (i + 1) % 4) for i in range(4)]
DOWN = [(i, (i - 1) % 4) for i in range(4)]
SWAP = [(0, 1), (1, 0)]
LOWP = jnp.bfloat16


def up(a):
    return lax.ppermute(a, "z", UP)


def down(a):
    return lax.ppermute(a, "z", DOWN)


def across(a):
    return lax.ppermute(a, "yl", SWAP)


def phase(*arrays):
    return lax.optimization_barrier(arrays)


def gather(own, aside=None, needed=None):
    half = own.shape[0] // 2
    b0, am, ap = phase(across(own), up(own), down(own))
    bm, a2, bp, needed = phase(up(b0), down(ap), across(ap), needed(b0) if needed else ())
    other = [] if aside is None else [across(after(aside, bm))]
    low, high, *other = phase(up(bm[:half]), down(bp[half:]), *other)
    return [own, b0, ap, bp, a2, low, high, am, bm], other, needed


def add(*parts):
    total = parts[0].astype(F32)
    for part in parts[1:]:
        total = total + part.astype(F32)
    return total


def scatter(*lists, one=(), two=None, late=None):
    half = lists[0][0].shape[0] // 2
    steps = [(down(b2[:half]), up(b2[half:])) for _, _, _, _, _, b2, _, _ in lists]
    steps, one = phase(steps, one)
    held = []
    for (a0, b0, ap, bp, a2, _, am, bm), (r1, r2) in zip(lists, steps):
        bm = add(bm, jnp.pad(r1, ((0, half), (0, 0)))).astype(LOWP)
        bp = add(bp, jnp.pad(r2, ((half, 0), (0, 0)))).astype(LOWP)
        bm, a2, bp, am = phase(bm, a2, bp, am)
        held.append((a0, b0, ap, am, down(bm), up(a2), across(bp)))
    if two:
        held, one = phase(held, two(one))
    else:
        (held,) = phase(held)
    sent = []
    for a0, b0, ap, am, q1, q2, q3 in held:
        b0, ap, am = phase(add(b0, q1).astype(LOWP), add(ap, q2, q3).astype(LOWP), am)
        sent.append((a0, across(b0), down(am), up(ap)))
    sent, one = phase(sent, late(one) if late else one)
    return [add(*parts) for parts in sent], one


def dot(a, b, ca, cb):
    return lax.dot_general(a, b, (((ca,), (cb,)), ((), ())), preferred_element_type=F32)


def rms(v):
    return lax.rsqrt(jnp.mean(v * v, -1, keepdims=True) + EPS)


def norm_back(values, scale, cube, gain, d_normed):
    weighted = d_normed * gain
    d_gain = jnp.sum(d_normed * values * scale, 0)
    d_values = scale * weighted - values * cube * jnp.mean(weighted * values, -1, keepdims=True)
    return d_values, d_gain


def ffn_kernel(at, *refs):
    pieces, (grad_ref, gate_w, up_w, down_w) = refs[:-16], refs[-16:-12]
    rows_ref, inner_ref, dgu_ref = refs[-12:-9]
    outs, total = refs[-9:-1], refs[-1]
    step = pl.program_id(0)
    quarter = grad_ref.shape[0] // 4

    @pl.when(step == 0)
    def _():
        first = 0
        for piece in pieces:
            rows_ref[first : first + piece.shape[0], :] = piece[...]
            first += piece.shape[0]

    rows = rows_ref[...]
    gate = dot(gate_w[...], rows, 1, 1)
    lift = dot(up_w[...], rows, 1, 1)
    for dz in range(4):
        lanes = slice(dz * quarter, (dz + 1) * quarter)
        place = pl.ds(pl.multiple_of(lax.rem(at[0] + dz, 4) * quarter, quarter), quarter)
        d_inner = dot(down_w[...], grad_ref[place, :], 1, 1)
        g, u = gate[:, lanes], lift[:, lanes]
        sigma = sigmoid(g)
        inner_ref[:, place] = (g * sigma * u).astype(LOWP)
        dgu_ref[0, :, lanes] = (d_inner * u * sigma * (1.0 + g * (1.0 - sigma))).astype(LOWP)
        dgu_ref[1, :, lanes] = (d_inner * g * sigma).astype(LOWP)
    both = dgu_ref[...].reshape(-1, dgu_ref.shape[2])
    weights = jnp.concatenate([gate_w[...], up_w[...]], axis=0)
    part = dot(both, weights, 0, 0)

    @pl.when(step == 0)
    def _():
        total[...] = part

    @pl.when(step == pl.num_programs(0) - 1)
    def _():
        size = outs[0].shape[0]
        done = total[...] + part
        for i, out in enumerate(outs):
            out[...] = done[i * size : (i + 1) * size].astype(LOWP)


def cost(microseconds):
    return pl.CostEstimate(flops=microseconds * 10**9, bytes_accessed=microseconds * 3 * 10**6, transcendentals=0)


def ffn_back(at, pieces, grad_rows, gate_up, down_proj):
    rows, features = grad_rows.shape
    units = down_proj.shape[0]
    tile = units // 2
    full = lambda shape: pl.BlockSpec(tuple(shape), lambda i, at: (0,) * len(shape))
    part = pl.BlockSpec((tile, features), lambda i, at: (i, 0))
    gate, lift = (pl.BlockSpec((None, tile, features), lambda i, at, k=k: (k, i, 0)) for k in range(2))
    lines = pl.BlockSpec((tile, rows), lambda i, at: (i, 0))
    pair = pl.BlockSpec((2, tile, rows), lambda i, at: (0, i, 0))
    slot = (rows // 8, features)
    return pl.pallas_call(
        ffn_kernel,
        grid_spec=pltpu.PrefetchScalarGridSpec(
            num_scalar_prefetch=1,
            grid=(2,),
            in_specs=[full(p.shape) for p in pieces] + [full(grad_rows.shape), gate, lift, part],
            out_specs=[full(grad_rows.shape), lines, pair] + [full(slot)] * 8,
            scratch_shapes=[pltpu.VMEM((rows, features), F32)],
        ),
        out_shape=[jax.ShapeDtypeStruct(grad_rows.shape, LOWP)]
        + [jax.ShapeDtypeStruct((units, rows), LOWP)]
        + [jax.ShapeDtypeStruct((2, units, rows), LOWP)]
        + [jax.ShapeDtypeStruct(slot, LOWP)] * 8,
        compiler_params=pltpu.CompilerParams(vmem_limit_bytes=60 * 2**20),
        cost_estimate=cost(28),
        name="ffn",
    )(at, *pieces, grad_rows, gate_up, gate_up, down_proj)


def ffn_grads_kernel(at, dgu_ref, inner_ref, rows_ref, grad_ref, *refs):
    out_ref = refs[-1]
    width = rows_ref.shape[1]
    for first, value in ((0, dot(dgu_ref[...], rows_ref[...], 1, 0)), (width, dot(inner_ref[...], grad_ref[...], 1, 0))):
        lanes = slice(first, first + value.shape[1])
        for ref in refs[:-1]:
            value = value + ref[:, lanes].astype(F32)
        out_ref[:, lanes] = value.astype(LOWP)


def ffn_grads(half, dgu, inner, rows, grad_rows, *came):
    units, count = inner.shape
    tile = units // 4
    features = rows.shape[1]
    out = pl.BlockSpec((tile, features + features // 2), lambda i, at: (i, 0))
    return pl.pallas_call(
        ffn_grads_kernel,
        grid_spec=pltpu.PrefetchScalarGridSpec(
            num_scalar_prefetch=1,
            grid=(4,),
            in_specs=[
                pl.BlockSpec((None, tile, count), lambda i, at: (at[0], i, 0)),
                pl.BlockSpec((tile, count), lambda i, at: (2 * at[0] + i % 2, 0)),
                pl.BlockSpec(rows.shape, lambda i, at: (0, 0)),
                pl.BlockSpec((count, features // 2), lambda i, at: (0, i // 2)),
            ]
            + [out] * len(came),
            out_specs=out,
        ),
        out_shape=jax.ShapeDtypeStruct((units, features + features // 2), LOWP),
        compiler_params=pltpu.CompilerParams(vmem_limit_bytes=48 * 2**20),
        cost_estimate=cost(9),
        name="ffn_grads",
    )(half, dgu, inner, rows, grad_rows, *came)


def place_ffn_kernel(where, own_ref, other_ref, two_ref, down_ref):
    def write(ref):
        width = two_ref.shape[1]
        two_ref[...] = ref[:, :width].astype(F32)
        down_ref[...] = ref[:, width:].astype(F32)

    pl.when(pl.program_id(0) < 4)(lambda: write(own_ref))
    pl.when(pl.program_id(0) >= 4)(lambda: write(other_ref))


def place_ffn(where, own, other, units, features):
    tile = units // 4
    core = lambda i, at: (at[0] + i // 4) % 2
    part = lambda i, at: i % 4
    return pl.pallas_call(
        place_ffn_kernel,
        grid_spec=pltpu.PrefetchScalarGridSpec(
            num_scalar_prefetch=1,
            grid=(8,),
            in_specs=[
                pl.BlockSpec((tile, own.shape[1]), lambda i, at: (jnp.minimum(i, 3), 0)),
                pl.BlockSpec((tile, own.shape[1]), lambda i, at: (jnp.maximum(i - 4, 0), 0)),
            ],
            out_specs=[
                pl.BlockSpec((None, tile, features), lambda i, at: (core(i, at), part(i, at), 0)),
                pl.BlockSpec((tile, features // 2), lambda i, at: (2 * core(i, at) + part(i, at) % 2, part(i, at) // 2)),
            ],
        ),
        out_shape=[jax.ShapeDtypeStruct((2, units, features), F32), jax.ShapeDtypeStruct((units, features), F32)],
        compiler_params=pltpu.CompilerParams(vmem_limit_bytes=32 * 2**20),
        cost_estimate=cost(9),
        name="place_ffn",
    )(where, own, other)


def grads_kernel(at, rows_ref, proj_ref, mixed_ref, attn_ref, *refs):
    came = refs[: (len(refs) - 1) // 6]
    outs, turn = refs[len(came) : -1], refs[-1]
    step = pl.program_id(0)
    turn[...] = dot(mixed_ref[...], attn_ref[...], 0, 0)
    size = turn.shape[0] // 2
    part = turn[pl.ds(pl.multiple_of(lax.rem(at[1] + step, 2) * size, size), size), :]
    value = jnp.concatenate([dot(rows_ref[...], proj_ref[...], 0, 0), part], axis=0)
    for ref in came:
        value = value + ref[...].astype(F32)
    value = value.astype(LOWP)
    if len(outs) == 1:
        outs[0][...] = value
        return
    half = value.shape[0] // 2

    def write(*pairs):
        for out, part in pairs:
            out[...] = part

    pl.when(step == 0)(lambda: write((outs[0], value)))
    pl.when(step == 1)(lambda: write((outs[1], value)))
    pl.when(step == 2)(lambda: write((outs[2], value[:half]), (outs[3], value[half:])))
    pl.when(step == 3)(lambda: write((outs[4], value)))


def mixer_grads(where, rows, d_mixed, mixer_rows, grad_attn, *came):
    features, width = rows.shape[1], 4 * WIDTH
    tile = features // 8
    heads = mixer_rows.shape[1] // 2
    size = tile + heads // 2
    part = lambda i, at: lax.rem(at[1] + i, 4)
    stacked = pl.BlockSpec((None, size, width), lambda i, at: (i, 0, 0))
    if came:
        sizes = [size, size, size // 2, size // 2, size]
        out_specs = [pl.BlockSpec((n, width), lambda i, at: (0, 0)) for n in sizes]
        out_shape = [jax.ShapeDtypeStruct((n, width), LOWP) for n in sizes]
    else:
        out_specs, out_shape = stacked, jax.ShapeDtypeStruct((4, size, width), LOWP)
    return pl.pallas_call(
        grads_kernel,
        grid_spec=pltpu.PrefetchScalarGridSpec(
            num_scalar_prefetch=1,
            grid=(4,),
            in_specs=[
                pl.BlockSpec((rows.shape[0], tile), lambda i, at: (0, at[0] * 4 + part(i, at))),
                pl.BlockSpec((rows.shape[0], width), lambda i, at: (0, 0)),
                pl.BlockSpec((rows.shape[0], heads), lambda i, at: (0, at[0])),
                pl.BlockSpec((rows.shape[0], width), lambda i, at: (0, part(i, at) // 2)),
            ]
            + [stacked] * len(came),
            out_specs=out_specs,
            scratch_shapes=[pltpu.VMEM((heads, width), F32)],
        ),
        out_shape=out_shape,
        compiler_params=pltpu.CompilerParams(vmem_limit_bytes=48 * 2**20),
        cost_estimate=cost(8),
        name="mixer_grads",
    )(where, rows, d_mixed, mixer_rows, grad_attn, *came)


def place_kernel(order, *refs):
    out_ref, low_ref = refs[-2:]
    parts = refs[:-2]
    width, tile = out_ref.shape[2], out_ref.shape[0]
    step = pl.program_id(0)

    def write(*group):
        value = jnp.concatenate([ref[...] for ref in group], axis=0) if len(group) > 1 else group[0][...]
        for k in range(out_ref.shape[1]):
            out_ref[:, k, :] = value[:tile, k * width : (k + 1) * width].astype(F32)
        low_ref[...] = value[tile:].astype(F32)

    at = 0
    done = 0
    while at < len(parts):
        size = tile + low_ref.shape[0]
        group = parts[at : at + (1 if parts[at].shape[0] == size else 2)]
        pl.when(step == done)(lambda group=group: write(*group))
        at, done = at + len(group), done + 1


def place_rows(where, parts, eighth, shape, low, *rest):
    rows = shape[0] // 8
    size = rows + low[0] // 4
    full = lambda a: pl.BlockSpec(a.shape, lambda i, at: (0, 0))
    steps = sum(p.shape[0] for p in parts) // size
    core = lambda i, at: lax.rem(eighth(i, at)[0], 2)
    x = lambda i, at: lax.rem(eighth(i, at)[1], 4)
    return pl.pallas_call(
        place_kernel if not rest else lambda at, *refs: place_kernel(at, *refs[: len(parts)], *refs[-2:]),
        grid_spec=pltpu.PrefetchScalarGridSpec(
            num_scalar_prefetch=1,
            grid=(steps,),
            in_specs=[full(p) for p in parts] + [pl.BlockSpec(memory_space=pl.ANY)] * len(rest),
            out_specs=[
                pl.BlockSpec((rows,) + shape[1:], lambda i, at: (4 * core(i, at) + x(i, at), 0, 0)),
                pl.BlockSpec((size - rows, low[1] // 2), lambda i, at: (2 * core(i, at) + lax.rem(x(i, at), 2), x(i, at) // 2)),
            ],
        ),
        out_shape=[jax.ShapeDtypeStruct(shape, F32), jax.ShapeDtypeStruct(low, F32)],
        input_output_aliases={1 + len(parts) + i: i for i in range(len(rest))},
        cost_estimate=cost(5),
        name="place_rows",
    )(where, *parts, *rest)


def after(value, *others):
    return lax.optimization_barrier((value, others))[0]


def over_yh(part):
    return add(part, lax.ppermute(part, "yh", SWAP)).astype(LOWP)


def butterfly(value, axis, size):
    step = 1
    while step < size:
        value = value + lax.ppermute(value, axis, [(i, i ^ step) for i in range(size)])
        step *= 2
    return value


def shards(
    tokens, lengths, cotangent, attn_gain, mixer_in, rate_proj, conv_weight, decay_rate, decay_bias,
    out_gain, out_proj, ffn_gain, gate_up, down_proj,
):
    rows = tokens.shape[2]
    micros = tokens.shape[1]
    z, yl = lax.axis_index("z"), lax.axis_index("yl")
    places = (2 * z + yl) * rows + jnp.arange(rows, dtype=jnp.int32)
    block = jnp.arange(8, dtype=jnp.int32)
    slots = 2 * ((block // 2 - z) % 4) + (block % 2 + yl) % 2

    width = mixer_in.shape[1] * mixer_in.shape[2]
    both_in = gate_up.transpose(1, 2, 0)
    dec = jnp.pad(jnp.stack([decay_rate, decay_bias]), ((0, 0), (0, 126)))
    gain_row = out_gain[None]

    source = tokens[0].astype(F32).reshape(-1, tokens.shape[3])
    valid = jnp.concatenate([(places < lengths[0, m]).astype(F32)[:, None] for m in range(micros)], axis=0)
    scale_one = rms(source)
    grad_out = cotangent[0].astype(F32).reshape(source.shape) * valid
    grad_low = grad_out.astype(LOWP)
    swap = lambda a: lax.ppermute(a, "c", SWAP)
    scatter_x = lambda a: lax.psum_scatter(a, "x", scatter_dimension=0, tiled=True)
    core, x = lax.axis_index("c"), lax.axis_index("x")
    where, elsewhere = jnp.stack([core, x]), jnp.stack([1 - core, x])

    normed = (source * scale_one * attn_gain).astype(LOWP)

    def weights(start):
        parts, rates = after((mixer_in, rate_proj), start)
        rates = jnp.pad(rates.reshape(rates.shape[0], 4), ((0, 0), (0, 124)))
        return jnp.concatenate([parts.reshape(parts.shape[0], width), rates], axis=1)

    pieces, (grad_other,), w_in = gather(normed, grad_low, weights)
    pieces = after(pieces, grad_other)
    grad_rows = lax.all_gather(jnp.concatenate([grad_low, grad_other], axis=0), "z", axis=0, tiled=True)

    sums, (rows_one, mixed, mixer_rows), saved = mixer_fwd(
        slots, pieces, w_in, conv_weight, dec, gain_row, out_proj, micros
    )
    (attended,), grad_rows = scatter(sums, two=lambda _: grad_rows)
    hidden = source + attended
    scale_two = rms(hidden)
    pieces, _, _ = gather((hidden * scale_two * ffn_gain).astype(LOWP))

    rows_two, inner, dgu, *parts = ffn_back(z[None], pieces, grad_rows, both_in, down_proj)
    half_of = lambda where, inner, *came: ffn_grads(where, dgu, inner, rows_two, grad_rows, *came)
    (d_normed,), d_ffn = scatter(
        parts,
        one=half_of(elsewhere, inner),
        two=swap,
        late=lambda came: half_of(where, inner, came),
    )
    d_ffn = scatter_x(d_ffn)
    d_from, d_ffn_gain = norm_back(hidden, scale_two, scale_two**3, ffn_gain, d_normed)
    d_hidden = grad_out + d_from
    branch = dot(inner, down_proj, 0, 0).astype(LOWP)
    pieces, _, branch = gather(d_hidden.astype(LOWP), None, lambda _: branch)
    pieces, d_ffn = phase(pieces, d_ffn)
    d_ffn = over_yh(d_ffn)

    grad_attn, d_mixed, d_conv, d_small = mixer_bwd(
        slots, pieces, mixed, conv_weight, dec, gain_row, out_proj, saved, micros
    )
    d_mixed, d_ffn = phase(d_mixed, d_ffn)
    half_of = lambda where, *came: mixer_grads(
        where, *(a.reshape(-1, a.shape[2]) for a in (rows_one, d_mixed, mixer_rows, grad_attn)), *came
    )
    x_up, x_down = (lambda a: lax.ppermute(a, "x", UP)), (lambda a: lax.ppermute(a, "x", DOWN))
    d_ffn = lax.all_gather(d_ffn, "x", axis=0, tiled=True)
    came, parts = phase(swap(half_of(elsewhere)), normed_grad(slots, d_mixed, w_in))

    def far(kept):
        p0, p1, p2, p2_end, p3 = kept
        r1, r3 = x_up(p2), x_down(p2_end)
        return p0, p1, r1, p3, r3

    def near(kept):
        p0, p1, r1, p3, r3 = kept
        half = r1.shape[0]
        p1 = add(p1, jnp.pad(r1, ((0, half), (0, 0)))).astype(LOWP)
        p3 = add(p3, jnp.pad(r3, ((half, 0), (0, 0)))).astype(LOWP)
        d_rate = dot(d_mixed[:, :, width:].reshape(-1, 128), rows_one.reshape(-1, rows_one.shape[2]), 0, 0)[:4]
        return (p0, x_up(p1), x_down(p3)), d_ffn, (d_rate, d_conv.sum(0), d_small.sum(0), scale_one**3)

    (d_normed,), (kept, d_ffn, (d_rate, d_conv, d_small, cube_one)) = scatter(parts, one=half_of(where, came), two=far, late=near)
    own = add(*kept).astype(LOWP)
    branch, own = phase(branch, own)
    branch = lax.psum_scatter(after(branch, d_ffn), "z", scatter_dimension=0, tiled=True)
    d_from, d_attn_gain = norm_back(source, scale_one, cube_one, attn_gain, d_normed)
    d_tokens = (d_hidden + d_from).astype(LOWP)
    flat = [d_rate, d_conv, d_small[:2], d_attn_gain, d_ffn_gain, d_small[2]]
    sizes = [a.size for a in flat]
    small = jnp.concatenate([a.reshape(-1) for a in flat]).reshape(-1, 128)
    came, d_ffn, small = phase(lax.ppermute(own, "yh", SWAP), (d_ffn, swap(d_ffn)), butterfly(butterfly(small, "c", 2), "x", 4))
    own = add(own, came).astype(LOWP)
    d_two, d_down = place_ffn(where, *d_ffn, dgu.shape[1], rows_two.shape[1])
    p3, p1, own_other, small, d_two, d_down, d_tokens = phase(
        x_up(own), x_down(own), swap(own), butterfly(small, "yh", 2), d_two, d_down, d_tokens
    )
    rates_end = sum(sizes[:3])
    half = own.shape[0] // 2
    shape, low = mixer_in.shape, out_proj.shape
    placed = place_rows(where, [own, p1, p3], lambda i, at: (at[0], at[1] + i + i // 2), shape, low)
    low_half, high_half, p1_other, p3_other, gains, branch, placed = phase(
        x_down(p1[:half]), x_up(p3[half:]), swap(p1), swap(p3), butterfly(small[rates_end // 128 :], "yl", 2), branch, placed
    )
    half = branch.shape[0] // 2
    gains, small, came, low_other, high_other, placed = phase(
        butterfly(gains, "z", 4),
        small,
        across(branch[half:]),
        swap(low_half),
        swap(high_half),
        place_rows(
            where, [own_other, p1_other, p3_other], lambda i, at: (at[0] + 1, at[1] + i + i // 2), shape, low, *placed
        ),
    )
    branch = add(branch[:half], came)
    layer_out = ((hidden + branch) * valid).astype(LOWP)
    last = [low_half, high_half, low_other, high_other]
    d_mixer_in, d_out = place_rows(where, last, lambda i, at: (at[0] + i, at[1] + 2), shape, low, *placed)
    gains = gains.reshape(-1)
    own = small.reshape(-1)[:rates_end]
    d_rate = own[: sizes[0]].reshape(2, 2, -1).transpose(2, 0, 1)
    d_conv = own[sizes[0] : sizes[0] + sizes[1]].reshape(conv_weight.shape)
    d_pair = own[sizes[0] + sizes[1] :].reshape(2, 128)
    return (
        layer_out.reshape(tokens.shape),
        d_tokens.reshape(tokens.shape),
        gains[: sizes[3]],
        d_mixer_in,
        d_rate,
        d_conv,
        d_pair[0, :2],
        d_pair[1, :2],
        gains[sizes[3] + sizes[4] :],
        d_out,
        gains[sizes[3] : sizes[3] + sizes[4]],
        d_two.transpose(2, 0, 1),
        d_down,
    )


def solution(mesh):
    fine = Mesh(mesh.devices.reshape(4, 2, 2, 4, 2), ("x", "yh", "c", "z", "yl"))
    dp, tensor = ("x", "yh", "c"), ("z", "yl")
    in_specs = (
        P(dp, None, tensor, None),
        P(dp, None),
        P(dp, None, tensor, None),
        P(),
        P(None, None, tensor),
        P(None, None, tensor),
        P(None, None, tensor),
        P(tensor),
        P(tensor),
        P(),
        P(tensor, None),
        P(),
        P(None, None, tensor),
        P(tensor, None),
    )
    out_specs = (
        P(dp, None, tensor, None),
        P(dp, None, tensor, None),
        P(),
        P(None, None, tensor),
        P(None, None, tensor),
        P(None, None, tensor),
        P(tensor),
        P(tensor),
        P(),
        P(tensor, None),
        P(),
        P(None, None, tensor),
        P(tensor, None),
    )
    return jax.shard_map(shards, mesh=fine, in_specs=in_specs, out_specs=out_specs, check_vma=False)
```

profile of v0, /device:TPU:1, one launch (start us, length us, event | category | flops | bytes accessed | tf_op | source)
XLA Modules:
  0.0 500.1 jit_solution(16988887711575482436)
XLA Ops:
  36.7 5.4 %collective-permute-done.3.refs_8_ = bf16[128,2048]{1,0:T(8,128)(2,1)S(1)} collective-permute-done((bf16[128,2048]{1,0:T(8,128)(2,1)}, bf16[128,2048]{1,0:T(8,128)(2,1)S(1)}, u32[]{:S(2)}, u32[]{:S(2)}) %collective-permute-start.3) | collective-permute-done | bytes 524320 | tf_op jit(solution)/shard_map/ppermute | solution.py:451
  54.7 33.1 %mixer_fwd.1 = (bf16[128,2048]{1,0:T(8,128)(2,1)}, bf16[128,2048]{1,0:T(8,128)(2,1)}, bf16[128,2048]{1,0:T(8,128)(2,1)}, bf16[128,2048]{1,0:T(8,128)(2,1)}, bf16...) custom-call(s32[8]{0:T(128)} %fusion.16.slots, ...), custom_call_target="tpu_custom_call" | custom-call | flops 30000001024 | bytes 90000000 | tf_op jit(solution)/shard_map/mixer_fwd/pallas_call | solution.py:360
  90.6 11.0 %collective-permute-done.9 = bf16[64,2048]{1,0:T(8,128)(2,1)S(1)} collective-permute-done((bf16[64,2048]{1,0:T(8,128)(2,1)S(1)}, bf16[64,2048]{1,0:T(8,128)(2,1)S(1)}, u32[]{:S(2)}, u32[]{:S(2)}) %collective-permute-start.9) | collective-permute-done | bytes 262176 | tf_op jit(solution)/shard_map/ppermute | solution.py:455
  108.1 8.4 %collective-permute-done.11 = bf16[128,2048]{1,0:T(8,128)(2,1)S(1)} collective-permute-done((bf16[128,2048]{1,0:T(8,128)(2,1)S(1)}, bf16[128,2048]{1,0:T(8,128)(2,1)S(1)}, u32[]{:S(2)}, u32[]{:S(2)}) %collective-permute-start.11) | collective-permute-done | bytes 524320 | tf_op jit(solution)/shard_map/ppermute | solution.py:455
  122.9 5.0 %collective-permute-done.14 = bf16[128,2048]{1,0:T(8,128)(2,1)S(1)} collective-permute-done((bf16[128,2048]{1,0:T(8,128)(2,1)S(1)}, bf16[128,2048]{1,0:T(8,128)(2,1)S(1)}, u32[]{:S(2)}, u32[]{:S(2)}) %collective-permute-start.14) | collective-permute-done | bytes 524320 | tf_op jit(solution)/shard_map/ppermute | solution.py:459
  137.5 6.1 %collective-permute-done.17.refs_1_ = bf16[128,2048]{1,0:T(8,128)(2,1)S(1)} collective-permute-done((bf16[128,2048]{1,0:T(8,128)(2,1)S(1)}, bf16[128,2048]{1,0:T(8,128)(2,1)S(1)}, u32[]{:S(2)}, u32[]{:S(2)}) %collective-permute-start.17) | collective-permute-done | bytes 524320 | tf_op jit(solution)/shard_map/ppermute | solution.py:459
  148.7 6.5 %collective-permute-done.20.refs_8_ = bf16[128,2048]{1,0:T(8,128)(2,1)S(1)} collective-permute-done((bf16[128,2048]{1,0:T(8,128)(2,1)S(1)}, bf16[128,2048]{1,0:T(8,128)(2,1)S(1)}, u32[]{:S(2)}, u32[]{:S(2)}) %collective-permute-start.20) | collective-permute-done | bytes 524320 | tf_op jit(solution)/shard_map/ppermute | solution.py:451
  165.0 27.3 %ffn.1 = (bf16[1024,2048]{1,0:T(8,128)(2,1)}, bf16[704,1024]{1,0:T(8,128)(2,1)}, bf16[2,704,1024]{2,1,0:T(8,128)(2,1)}, bf16[128,2048]{1,0:T(8,128)(2,1)}, bf16[...) custom-call(s32[1]{0:T(128)} %bitcast.8.at, ...), custom_call_target="tpu_custom_call" | custom-call | flops 28000000000 | bytes 84000000 | tf_op jit(solution)/shard_map/ffn/pallas_call | solution.py:575
  199.1 10.3 %ffn_grads.2 = bf16[704,3072]{1,0:T(8,128)(2,1)} custom-call(s32[2]{0:T(128)S(1)} %pad_add_fusion.at, bf16[2,704,1024]{2,1,0:T(8,128)(2,1)S(1)} %copy-done.9, bf16[704,1024]{1,0:T(8,128)(2,1)S(1)} %copy-done.10, bf16[1024,2048]{1,0:T(8,128)(2,1)} %get-tuple-element.305.rows_ref, bf16[1024,2048]{1,0:T(8,128)(2,1)} %all-gather.3.cloned.1.call-done.refs_9_.grad_ref), custom_call_target="tpu_custom_call" | custom-call | flops 8999999488 | bytes 27000000 | tf_op jit(solution)/shard_map/ffn_grads/pallas_call | solution.py:609
  209.4 8.8 %collective-permute-start.30 = (bf16[704,3072]{1,0:T(8,128)(2,1)}, bf16[704,3072]{1,0:T(8,128)(2,1)S(1)}, u32[]{:S(2)}, u32[]{:S(2)}) collective-permute-start(bf16[704,3072]{1,0:T(8,128)(2,1)} %ffn_grads.2), channel_id=1, source_target_pairs={{0,8},{8,0},{1,9},{9,1},{2,10},{10,2},{3,11},{11,3},{4,12},{12,4},... | collective-permute-start | bytes 12976136 | tf_op jit(solution)/shard_map/ppermute | solution.py:809
  222.7 10.1 %collective-permute-done.27 = bf16[128,2048]{1,0:T(8,128)(2,1)S(1)} collective-permute-done((bf16[128,2048]{1,0:T(8,128)(2,1)S(1)}, bf16[128,2048]{1,0:T(8,128)(2,1)S(1)}, u32[]{:S(2)}, u32[]{:S(2)}) %collective-permute-start.27) | collective-permute-done | bytes 524320 | tf_op jit(solution)/shard_map/ppermute | solution.py:455
  241.0 11.0 %ffn_grads.3 = bf16[704,3072]{1,0:T(8,128)(2,1)} custom-call(s32[2]{0:T(128)S(1)} %pad_add_fusion.1.at.where.order, bf16[2,704,1024]{2,1,0:T(8,128)(2,1)S(1)} %copy-done.9, bf16[704,1024]{1,0:T(8,128)(2,1)S(1)} %copy-done.10, bf16[1024,2048]{1,0:T(8,128)(2,1)} %get-tuple-element.305.rows_ref, ...), custom_call_target="tpu_custom_call" | custom-call | flops 8999999488 | bytes 27000000 | tf_op jit(solution)/shard_map/ffn_grads/pallas_call | solution.py:609
  261.3 7.6 %collective-permute-done.34.refs_1_ = bf16[128,2048]{1,0:T(8,128)(2,1)S(1)} collective-permute-done((bf16[128,2048]{1,0:T(8,128)(2,1)S(1)}, bf16[128,2048]{1,0:T(8,128)(2,1)S(1)}, u32[]{:S(2)}, u32[]{:S(2)}) %collective-permute-start.34) | collective-permute-done | bytes 524320 | tf_op jit(solution)/shard_map/ppermute | solution.py:459
  273.6 5.1 %convolution_convert_fusion = bf16[1024,2048]{1,0:T(8,128)(2,1)} fusion(bf16[704,1024]{1,0:T(8,128)(2,1)S(1)} %copy-done.11, bf16[704,2048]{1,0:T(8,128)(2,1)S(1)} %copy-done.57), kind=kOutput, calls=%fused_computation.3 | convolution fusion | flops 2954887168 | bytes 8519680 | tf_op jit(solution)/shard_map/dot_general | solution.py:505
  286.4 5.3 %collective-permute-done.40.refs_5_ = bf16[64,2048]{1,0:T(8,128)(2,1)S(1)} collective-permute-done((bf16[64,2048]{1,0:T(8,128)(2,1)S(1)}, bf16[64,2048]{1,0:T(8,128)(2,1)S(1)}, u32[]{:S(2)}, u32[]{:S(2)}) %collective-permute-start.40) | collective-permute-done | bytes 262176 | tf_op jit(solution)/shard_map/ppermute | solution.py:451
  291.7 10.9 %reduce-scatter.3.cloned.1.call-done = bf16[176,3072]{1,0:T(8,128)(2,1)} async-done(((bf16[704,3072]{1,0:T(8,128)(2,1)}), bf16[176,3072]{1,0:T(8,128)(2,1)}) %reduce-scatter.3.cloned.1.call-update) | async-done | bytes 1081360 | tf_op jit(solution)/shard_map/reduce_scatter | solution.py:810
  305.6 24.4 %mixer_bwd.1 = (bf16[2,512,2048]{2,1,0:T(8,128)(2,1)}, bf16[2,512,1152]{2,1,0:T(8,128)(2,1)}, f32[2,3,4,256]{3,2,1,0:T(4,128)}, f32[2,8,128]{2,1,0:T(8,128)}) custom-call(s32[8]{0:T(128)} %fusion.16.slots, bf16[128,2048]{1,0:T(8,128)(2,1)} %copy-done.25, bf16[128,2048]{1,0:T(8,128)(2,1)} %copy-done.65, bf16[128,2048]{1,0:T(8,128)(2,1)} %copy-done.67, ...), custom_call_target="tpu_custom_call" | custom-call | flops 32000000000 | bytes 96000000 | tf_op jit(solution)/shard_map/mixer_bwd/pallas_call | solution.py:360
  333.1 8.5 %mixer_grads.2 = bf16[4,320,1024]{2,1,0:T(8,128)(2,1)} custom-call(s32[2]{0:T(128)S(1)} %pad_add_fusion.at, bf16[1024,2048]{1,0:T(8,128)(2,1)} %bitcast.90, bf16[1024,1152]{1,0:T(8,128)(2,1)S(1)} %bitcast.84, bf16[1024,256]{1,0:T(8,128)(2,1)S(1)} %bitcast.86, bf16[1024,2048]{1,0:T(8,128)(2,1)} %bitcast.108), custom_call_target="tpu_custom_call" | custom-call | flops 8000000000 | bytes 24000000 | tf_op jit(solution)/shard_map/mixer_grads/pallas_call | solution.py:704
  342.6 10.2 %normed_grad.1 = (bf16[128,2048]{1,0:T(8,128)(2,1)S(1)}, bf16[128,2048]{1,0:T(8,128)(2,1)S(1)}, bf16[128,2048]{1,0:T(8,128)(2,1)S(1)}, bf16[128,2048]{1,0:T(8,12...) custom-call(s32[8]{0:T(128)S(1)} %copy-done.8, ...), custom_call_target="tpu_custom_call" | custom-call | flops 8000000000 | bytes 24000000 | tf_op jit(solution)/shard_map/normed_grad/pallas_call | solution.py:425
  356.1 8.9 %mixer_grads.3 = (bf16[320,1024]{1,0:T(8,128)(2,1)S(1)}, bf16[320,1024]{1,0:T(8,128)(2,1)S(1)}, bf16[160,1024]{1,0:T(8,128)(2,1)}, bf16[160,1024]{1,0:T(8,128)(2,1)}, bf16[320,1024]{1,0:T(8,128)(2,1)S(1)}) custom-call(s32[2]{0:T(128)S(1)} %pad_add_fusion.1.at.where.order, bf16[1024,2048]{1,0:T(8,128)(2,1)} %bitcast.91, bf16[1024,1152]{1,0:T(8,128)(2,1)S(1)} %bitcast.85, ...), custom_call_target="tpu_custom_call" | custom-call | flops 8000000000 | bytes 24000000 | tf_op jit(solution)/shard_map/mixer_grads/pallas_call | solution.py:704
  373.7 14.5 %collective-permute-done.49 = bf16[160,1024]{1,0:T(8,128)(2,1)} collective-permute-done((bf16[160,1024]{1,0:T(8,128)(2,1)}, bf16[160,1024]{1,0:T(8,128)(2,1)}, u32[]{:S(2)}, u32[]{:S(2)}) %collective-permute-start.49) | collective-permute-done | bytes 327712 | tf_op jit(solution)/shard_map/ppermute | solution.py:856
  450.2 7.2 %place_ffn.1 = (f32[2,704,2048]{2,1,0:T(8,128)}, f32[704,2048]{1,0:T(8,128)}) custom-call(s32[2]{0:T(128)S(1)} %pad_add_fusion.1.at.where.order, bf16[704,3072]{1,0:T(8,128)(2,1)S(1)} %copy-done.2, bf16[704,3072]{1,0:T(8,128)(2,1)S(1)} %collective-permute-done.57.other_ref), custom_call_target="tpu_custom_call" | custom-call | flops 8999999488 | bytes 27000000 | tf_op jit(solution)/shard_map/place_ffn/pallas_call | solution.py:644
  464.0 5.0 %place_rows.3 = (f32[2048,4,256]{2,1,0:T(4,128)}, f32[256,2048]{1,0:T(8,128)}) custom-call(s32[2]{0:T(128)} %copy-done.7, bf16[320,1024]{1,0:T(8,128)(2,1)} %copy-done.24, bf16[320,1024]{1,0:T(8,128)(2,1)} %copy-done.36, bf16[320,1024]{1,0:T(8,128)(2,1)} %copy-done.35), custom_call_target="tpu_custom_call" | custom-call | flops 5000000000 | bytes 15000000 | tf_op jit(solution)/shard_map/place_rows/pallas_call | solution.py:754
  478.3 5.0 %place_rows.4 = (f32[2048,4,256]{2,1,0:T(4,128)}, f32[256,2048]{1,0:T(8,128)}) custom-call(s32[2]{0:T(128)} %copy-done.7, bf16[320,1024]{1,0:T(8,128)(2,1)} %copy-done.58, bf16[320,1024]{1,0:T(8,128)(2,1)} %collective-permute-done.67.refs_1_, bf16[320,1024]{1,0:T(8,128)(2,1)} %collective-permute-done.68.refs_2_, ...), custom_call_target="tpu_custom_call", output_to_operand_aliasing={{0}: (4, {}), {1}: (5, {})} | custom-call | flops 5000000000 | bytes 15000000 | tf_op jit(solution)/shard_map/place_rows/pallas_call | solution.py:754
  (392 shorter events, 229.5 us)
Async XLA Ops:
  7.2 109.4 %all-gather.3.cloned.1.call-start = ((), (), s32[]{:S(2)}) async-start(), calls=%async_computation.2 | async-start | bytes 5242880 | tf_op jit(solution)/shard_map/all_gather | solution.py:823
  12.0 15.1 %collective-permute-start.1 = (bf16[128,2048]{1,0:T(8,128)(2,1)S(1)}, bf16[128,2048]{1,0:T(8,128)(2,1)S(1)}, u32[]{:S(2)}, u32[]{:S(2)}) collective-permute-start(bf16[128,2048]{1,0:T(8,128)(2,1)S(1)} %fusion.6.refs_0_), channel_id=1, source_target_pairs={{0,2},{2,4},{4,6},{6,0},{1,3},{3,5},{5,7},{7,1},{8,10},{10,12},{12... | collective-permute-start | bytes 1572872 | tf_op jit(solution)/shard_map/ppermute | solution.py:451
  27.1 15.0 %collective-permute-start.4 = (bf16[128,2048]{1,0:T(8,128)(2,1)}, bf16[128,2048]{1,0:T(8,128)(2,1)}, u32[]{:S(2)}, u32[]{:S(2)}) collective-permute-start(bf16[128,2048]{1,0:T(8,128)(2,1)} %collective-permute-done.2.refs_2_), channel_id=1, source_target_pairs={{0,6},{2,0},{4,2},{6,4},{1,7},{3,1},{5,3},{7,5},{8,14},{10,8},{12,... | collective-permute-start | bytes 1572872 | tf_op jit(solution)/shard_map/ppermute | solution.py:455
  53.4 249.3 %reduce-scatter.3.cloned.1.call-start = ((), (), s32[]{:S(2)}) async-start(), calls=%async_computation.3 | async-start | bytes 5406720 | tf_op jit(solution)/shard_map/reduce_scatter | solution.py:810
  193.4 16.0 %collective-permute-start.25 = (bf16[64,2048]{1,0:T(8,128)(2,1)S(1)}, bf16[64,2048]{1,0:T(8,128)(2,1)S(1)}, u32[]{:S(2)}, u32[]{:S(2)}) collective-permute-start(bf16[64,2048]{1,0:T(8,128)(2,1)S(1)} %get-tuple-element.474), channel_id=1, source_target_pairs={{0,6},{2,0},{4,2},{6,4},{1,7},{3,1},{5,3},{7,5},{8,14},{10,8},{12,... | collective-permute-start | bytes 786440 | tf_op jit(solution)/shard_map/ppermute | solution.py:455
  209.4 26.5 %collective-permute-start.30 = (bf16[704,3072]{1,0:T(8,128)(2,1)}, bf16[704,3072]{1,0:T(8,128)(2,1)S(1)}, u32[]{:S(2)}, u32[]{:S(2)}) collective-permute-start(bf16[704,3072]{1,0:T(8,128)(2,1)} %ffn_grads.2), channel_id=1, source_target_pairs={{0,8},{8,0},{1,9},{9,1},{2,10},{10,2},{3,11},{11,3},{4,12},{12,4},... | collective-permute-start | bytes 12976136 | tf_op jit(solution)/shard_map/ppermute | solution.py:809
  218.5 14.4 %collective-permute-start.27 = (bf16[128,2048]{1,0:T(8,128)(2,1)S(1)}, bf16[128,2048]{1,0:T(8,128)(2,1)S(1)}, u32[]{:S(2)}, u32[]{:S(2)}) collective-permute-start(bf16[128,2048]{1,0:T(8,128)(2,1)S(1)} %add_convert_fusion.12), channel_id=1, source_target_pairs={{0,6},{2,0},{4,2},{6,4},{1,7},{3,1},{5,3},{7,5},{8,14},{10,8},{12,... | collective-permute-start | bytes 1572872 | tf_op jit(solution)/shard_map/ppermute | solution.py:455
  221.5 14.4 %collective-permute-start.28 = (bf16[128,2048]{1,0:T(8,128)(2,1)S(1)}, bf16[128,2048]{1,0:T(8,128)(2,1)S(1)}, u32[]{:S(2)}, u32[]{:S(2)}) collective-permute-start(bf16[128,2048]{1,0:T(8,128)(2,1)S(1)} %copy-done.68), channel_id=1, source_target_pairs={{0,2},{2,4},{4,6},{6,0},{1,3},{3,5},{5,7},{7,1},{8,10},{10,12},{12... | collective-permute-start | bytes 1572872 | tf_op jit(solution)/shard_map/ppermute | solution.py:451
  221.5 14.4 %collective-permute-start.29 = (bf16[128,2048]{1,0:T(8,128)(2,1)S(1)}, bf16[128,2048]{1,0:T(8,128)(2,1)S(1)}, u32[]{:S(2)}, u32[]{:S(2)}) collective-permute-start(bf16[128,2048]{1,0:T(8,128)(2,1)S(1)} %add_convert_fusion.11), channel_id=1, source_target_pairs={{0,1},{1,0},{2,3},{3,2},{4,5},{5,4},{6,7},{7,6},{8,9},{9,8},{10,11... | collective-permute-start | bytes 1572872 | tf_op jit(solution)/shard_map/ppermute | solution.py:459
  253.7 159.7 %all-gather.5.cloned.1.call-start = ((), (), s32[]{:S(2)}) async-start(), calls=%async_computation.4 | async-start | bytes 5406720 | tf_op jit(solution)/shard_map/all_gather | solution.py:857
  302.7 27.4 %collective-permute-start.42 = (bf16[176,3072]{1,0:T(8,128)(2,1)}, bf16[176,3072]{1,0:T(8,128)(2,1)}, u32[]{:S(2)}, u32[]{:S(2)}) collective-permute-start(bf16[176,3072]{1,0:T(8,128)(2,1)} %reduce-scatter.3.cloned.1.call-done), channel_id=1, source_target_pairs={{0,16},{16,0},{1,17},{17,1},{2,18},{18,2},{3,19},{19,3},{4,20},{20... | collective-permute-start | bytes 3244040 | tf_op jit(solution)/shard_map/ppermute | solution.py:777
  342.6 130.1 %reduce-scatter.5.cloned.1.call-start = ((), (), s32[]{:S(2)}) async-start(), calls=%async_computation.5 | async-start | bytes 5242880 | tf_op jit(solution)/shard_map/reduce_scatter | solution.py:876
  366.7 21.4 %collective-permute-start.46 = (bf16[128,2048]{1,0:T(8,128)(2,1)}, bf16[128,2048]{1,0:T(8,128)(2,1)}, u32[]{:S(2)}, u32[]{:S(2)}) collective-permute-start(bf16[128,2048]{1,0:T(8,128)(2,1)} %add_convert_fusion.8), channel_id=1, source_target_pairs={{0,6},{2,0},{4,2},{6,4},{1,7},{3,1},{5,3},{7,5},{8,14},{10,8},{12,... | collective-permute-start | bytes 1572872 | tf_op jit(solution)/shard_map/ppermute | solution.py:455
  369.3 18.8 %collective-permute-start.47 = (bf16[128,2048]{1,0:T(8,128)(2,1)}, bf16[128,2048]{1,0:T(8,128)(2,1)}, u32[]{:S(2)}, u32[]{:S(2)}) collective-permute-start(bf16[128,2048]{1,0:T(8,128)(2,1)} %get-tuple-element.389), channel_id=1, source_target_pairs={{0,2},{2,4},{4,6},{6,0},{1,3},{3,5},{5,7},{7,1},{8,10},{10,12},{12... | collective-permute-start | bytes 1572872 | tf_op jit(solution)/shard_map/ppermute | solution.py:451
  369.3 18.8 %collective-permute-start.48 = (bf16[128,2048]{1,0:T(8,128)(2,1)}, bf16[128,2048]{1,0:T(8,128)(2,1)}, u32[]{:S(2)}, u32[]{:S(2)}) collective-permute-start(bf16[128,2048]{1,0:T(8,128)(2,1)} %add_convert_fusion.7), channel_id=1, source_target_pairs={{0,1},{1,0},{2,3},{3,2},{4,5},{5,4},{6,7},{7,6},{8,9},{9,8},{10,11... | collective-permute-start | bytes 1572872 | tf_op jit(solution)/shard_map/ppermute | solution.py:459
  370.4 17.7 %collective-permute-start.49 = (bf16[160,1024]{1,0:T(8,128)(2,1)}, bf16[160,1024]{1,0:T(8,128)(2,1)}, u32[]{:S(2)}, u32[]{:S(2)}) collective-permute-start(bf16[160,1024]{1,0:T(8,128)(2,1)} %get-tuple-element.393), channel_id=1, source_target_pairs={{0,32},{32,64},{64,96},{96,0},{1,33},{33,65},{65,97},{97,1},{2,34}... | collective-permute-start | bytes 983048 | tf_op jit(solution)/shard_map/ppermute | solution.py:856
  370.4 17.7 %collective-permute-start.50 = (bf16[160,1024]{1,0:T(8,128)(2,1)}, bf16[160,1024]{1,0:T(8,128)(2,1)}, u32[]{:S(2)}, u32[]{:S(2)}) collective-permute-start(bf16[160,1024]{1,0:T(8,128)(2,1)} %get-tuple-element.395), channel_id=1, source_target_pairs={{0,96},{32,0},{64,32},{96,64},{1,97},{33,1},{65,33},{97,65},{2,98}... | collective-permute-start | bytes 983048 | tf_op jit(solution)/shard_map/ppermute | solution.py:856
  390.1 23.4 %collective-permute-start.54 = (bf16[320,1024]{1,0:T(8,128)(2,1)}, bf16[320,1024]{1,0:T(8,128)(2,1)}, u32[]{:S(2)}, u32[]{:S(2)}) collective-permute-start(bf16[320,1024]{1,0:T(8,128)(2,1)} %add_convert_fusion.4), channel_id=1, source_target_pairs={{0,32},{32,64},{64,96},{96,0},{1,33},{33,65},{65,97},{97,1},{2,34}... | collective-permute-start | bytes 1966088 | tf_op jit(solution)/shard_map/ppermute | solution.py:856
  392.2 21.3 %collective-permute-start.55 = (bf16[320,1024]{1,0:T(8,128)(2,1)}, bf16[320,1024]{1,0:T(8,128)(2,1)}, u32[]{:S(2)}, u32[]{:S(2)}) collective-permute-start(bf16[320,1024]{1,0:T(8,128)(2,1)} %add_convert_fusion.3), channel_id=1, source_target_pairs={{0,96},{32,0},{64,32},{96,64},{1,97},{33,1},{65,33},{97,65},{2,98}... | collective-permute-start | bytes 1966088 | tf_op jit(solution)/shard_map/ppermute | solution.py:856
  415.9 25.0 %collective-permute-start.57 = (bf16[704,3072]{1,0:T(8,128)(2,1)}, bf16[704,3072]{1,0:T(8,128)(2,1)S(1)}, u32[]{:S(2)}, u32[]{:S(2)}) collective-permute-start(bf16[704,3072]{1,0:T(8,128)(2,1)} %all-gather.5.cloned.1.call-done.own_ref), channel_id=1, source_target_pairs={{0,8},{8,0},{1,9},{9,1},{2,10},{10,2},{3,11},{11,3},{4,12},{12,4},... | collective-permute-start | bytes 12976136 | tf_op jit(solution)/shard_map/ppermute | solution.py:809
  423.1 17.8 %collective-permute-start.56 = (bf16[320,1024]{1,0:T(8,128)(2,1)S(1)}, bf16[320,1024]{1,0:T(8,128)(2,1)S(1)}, u32[]{:S(2)}, u32[]{:S(2)}) collective-permute-start(bf16[320,1024]{1,0:T(8,128)(2,1)S(1)} %add_convert_fusion.2), channel_id=1, source_target_pairs={{0,16},{16,0},{1,17},{17,1},{2,18},{18,2},{3,19},{19,3},{4,20},{20... | collective-permute-start | bytes 1966088 | tf_op jit(solution)/shard_map/ppermute | solution.py:882
  441.2 16.8 %collective-permute-start.61 = (bf16[320,1024]{1,0:T(8,128)(2,1)S(1)}, bf16[320,1024]{1,0:T(8,128)(2,1)S(1)}, u32[]{:S(2)}, u32[]{:S(2)}) collective-permute-start(bf16[320,1024]{1,0:T(8,128)(2,1)S(1)} %add_convert_fusion.1.refs_0_), channel_id=1, source_target_pairs={{0,32},{32,64},{64,96},{96,0},{1,33},{33,65},{65,97},{97,1},{2,34}... | collective-permute-start | bytes 1966088 | tf_op jit(solution)/shard_map/ppermute | solution.py:856
  441.3 16.7 %collective-permute-start.62 = (bf16[320,1024]{1,0:T(8,128)(2,1)S(1)}, bf16[320,1024]{1,0:T(8,128)(2,1)S(1)}, u32[]{:S(2)}, u32[]{:S(2)}) collective-permute-start(bf16[320,1024]{1,0:T(8,128)(2,1)S(1)} %add_convert_fusion.1.refs_0_), channel_id=1, source_target_pairs={{0,96},{32,0},{64,32},{96,64},{1,97},{33,1},{65,33},{97,65},{2,98}... | collective-permute-start | bytes 1966088 | tf_op jit(solution)/shard_map/ppermute | solution.py:856
  458.0 14.6 %collective-permute-start.67 = (bf16[320,1024]{1,0:T(8,128)(2,1)S(1)}, bf16[320,1024]{1,0:T(8,128)(2,1)}, u32[]{:S(2)}, u32[]{:S(2)}) collective-permute-start(bf16[320,1024]{1,0:T(8,128)(2,1)S(1)} %collective-permute-done.62.refs_1_), channel_id=1, source_target_pairs={{0,8},{8,0},{1,9},{9,1},{2,10},{10,2},{3,11},{11,3},{4,12},{12,4},... | collective-permute-start | bytes 1966088 | tf_op jit(solution)/shard_map/ppermute | solution.py:809
  (133 other events, 2045.9 us)
Sparse Core Ops, SparseCore 0:
  53.5 57.6 all-gather.2
  253.8 48.7 reduce-scatter.2
  342.7 58.0 all-gather.4
  416.0 47.8 reduce-scatter.4
where the time goes:
time: 509 us; the launch traced here: 500 us
  waiting for transfers between devices  155 us (30%)
  Pallas kernels  155 us (30%)
  starting transfers between devices  104 us (20%)
  other arithmetic  41.9 us (8%)
  local copies, waits for them, and re-layouts  21.1 us (4%)
  between operations  15 us (3%)
  matrix products  8.13 us (2%)
    pallas_call x2, Pallas kernels, kernel_call(): pl.pallas_call(kernel, grid_spec=pltpu.PrefetchScalarGridSpec(num_scalar_...  57.5 us
    ppermute x18, waiting for transfers between devices, up(): return lax.ppermute(a, 'z', UP)  49.6 us
    ppermute x18, starting transfers between devices, down(): return lax.ppermute(a, 'z', DOWN)  39.4 us
    ppermute x18, waiting for transfers between devices, down(): return lax.ppermute(a, 'z', DOWN)  32.4 us
    ppermute x14, waiting for transfers between devices, across(): return lax.ppermute(a, 'yl', SWAP)  31.5 us
    pallas_call x1, Pallas kernels, ffn_back(): pl.pallas_call(ffn_kernel, grid_spec=pltpu.PrefetchScalarGridSpec(num_sca...  27.3 us
    pallas_call x2, Pallas kernels, ffn_grads(): pl.pallas_call(ffn_grads_kernel, grid_spec=pltpu.PrefetchScalarGridSpec(n...  21.3 us
    ppermute x8, starting transfers between devices, shards(): swap = lambda a: lax.ppermute(a, 'c', SWAP)  19.5 us
  transfers between devices with their start and end apart: 79, of which 36 were waited for; matrix products, arithmetic and copies ran while one was open for 9% of the time, Pallas kernels for 23%

commit v1 on v0

--- a/solution.py
+++ b/solution.py
@@ -15,6 +15,7 @@
 LOW = lax.Precision.DEFAULT
 P_INV = HIGH
 P_ST = HIGH
+P_OUT = LOW
 P_GR = HIGH
 P_BST = LOW
 P_BGR = LOW
@@ -200,10 +201,10 @@
             states.append(state)
     states = jnp.stack(states)
     state_ref[...] = states
-    seen = bdot(jnp.concatenate([solved[:, :, HS:], grow * queries], axis=1), states, 1, 0, P_ST)
+    seen = bdot(jnp.concatenate([solved[:, :, HS:], grow * queries], axis=1), states, 1, 0, P_OUT)
     errors = solved[:, :, :HS] - seen[:, :BLOCK]
     err_ref[...] = errors
-    outputs = seen[:, BLOCK:] + bdot(attend, errors, 1, 0, P_ST)
+    outputs = seen[:, BLOCK:] + bdot(attend, errors, 1, 0, P_OUT)
     out_ref[...] = outputs
     scale = lax.rsqrt(jnp.mean(outputs * outputs, -1, keepdims=True) + EPS)
     gate = proj_ref[:, 3 * width : 4 * width]
@@ -888,7 +889,9 @@
     rates_end = sum(sizes[:3])
     half = own.shape[0] // 2
     shape, low = mixer_in.shape, out_proj.shape
-    placed = place_rows(where, [own, p1, p3], lambda i, at: (at[0], at[1] + i + i // 2), shape, low)
+    placed = place_rows(
+        where, [own, p1, p3, own_other], lambda i, at: (at[0] + i // 3, at[1] + i + i // 2), shape, low
+    )
     low_half, high_half, p1_other, p3_other, gains, branch, placed = phase(
         x_down(p1[:half]), x_up(p3[half:]), swap(p1), swap(p3), butterfly(small[rates_end // 128 :], "yl", 2), branch, placed
     )
@@ -900,7 +903,7 @@
         swap(low_half),
         swap(high_half),
         place_rows(
-            where, [own_other, p1_other, p3_other], lambda i, at: (at[0] + 1, at[1] + i + i // 2), shape, low, *placed
+            where, [p1_other, p3_other], lambda i, at: (at[0] + 1, at[1] + 1 + 2 * i), shape, low, *placed
         ),
     )
     branch = add(branch[:half], came)

time: 509 us -> 509 us (level)
    unnamed x164 -> x166, local copies, waits for them, and re-layouts: 11.6 us -> 13.3 us
  transfers between devices with their start and end apart: 79 -> 79, of which waited for: 36 -> 34; matrix products, arithmetic and copies ran while one was open for 9% -> 9% of each run, Pallas kernels for 23% -> 23%
where the time goes in v1:
time: 509 us; the launch traced here: 502 us
  waiting for transfers between devices  157 us (31%)
  Pallas kernels  154 us (30%)
  starting transfers between devices  104 us (20%)
  other arithmetic  41.9 us (8%)
  local copies, waits for them, and re-layouts  22.8 us (4%)
  between operations  15 us (3%)
  matrix products  8.07 us (2%)
    pallas_call x2, Pallas kernels, kernel_call(): pl.pallas_call(kernel, grid_spec=pltpu.PrefetchScalarGridSpec(num_scalar_...  56.8 us
    ppermute x18, waiting for transfers between devices, up(): return lax.ppermute(a, 'z', UP)  48.4 us
    ppermute x18, starting transfers between devices, down(): return lax.ppermute(a, 'z', DOWN)  38.3 us
    ppermute x18, waiting for transfers between devices, down(): return lax.ppermute(a, 'z', DOWN)  34.5 us
    ppermute x14, waiting for transfers between devices, across(): return lax.ppermute(a, 'yl', SWAP)  32.7 us
    pallas_call x1, Pallas kernels, ffn_back(): pl.pallas_call(ffn_kernel, grid_spec=pltpu.PrefetchScalarGridSpec(num_sca...  27.3 us
    pallas_call x2, Pallas kernels, ffn_grads(): pl.pallas_call(ffn_grads_kernel, grid_spec=pltpu.PrefetchScalarGridSpec(n...  21.3 us
    ppermute x8, starting transfers between devices, shards(): swap = lambda a: lax.ppermute(a, 'c', SWAP)  19.4 us
  transfers between devices with their start and end apart: 79, of which 34 were waited for; matrix products, arithmetic and copies ran while one was open for 9% of the time, Pallas kernels for 23%

profile of v1, /device:TPU:1, one launch (start us, length us, event | category | flops | bytes accessed | tf_op | source)
XLA Modules:
  0.0 501.5 jit_solution(15426779358670103727)
XLA Ops:
  36.7 5.4 %collective-permute-done.3.refs_8_ = bf16[128,2048]{1,0:T(8,128)(2,1)S(1)} collective-permute-done((bf16[128,2048]{1,0:T(8,128)(2,1)}, bf16[128,2048]{1,0:T(8,128)(2,1)S(1)}, u32[]{:S(2)}, u32[]{:S(2)}) %collective-permute-start.3) | collective-permute-done | bytes 524320 | tf_op jit(solution)/shard_map/ppermute | solution.py:452
  54.7 32.4 %mixer_fwd.1 = (bf16[128,2048]{1,0:T(8,128)(2,1)}, bf16[128,2048]{1,0:T(8,128)(2,1)}, bf16[128,2048]{1,0:T(8,128)(2,1)}, bf16[128,2048]{1,0:T(8,128)(2,1)}, bf16...) custom-call(s32[8]{0:T(128)} %fusion.16.slots, ...), custom_call_target="tpu_custom_call" | custom-call | flops 30000001024 | bytes 90000000 | tf_op jit(solution)/shard_map/mixer_fwd/pallas_call | solution.py:361
  89.9 11.0 %collective-permute-done.9 = bf16[64,2048]{1,0:T(8,128)(2,1)S(1)} collective-permute-done((bf16[64,2048]{1,0:T(8,128)(2,1)S(1)}, bf16[64,2048]{1,0:T(8,128)(2,1)S(1)}, u32[]{:S(2)}, u32[]{:S(2)}) %collective-permute-start.9) | collective-permute-done | bytes 262176 | tf_op jit(solution)/shard_map/ppermute | solution.py:456
  107.4 9.9 %collective-permute-done.11 = bf16[128,2048]{1,0:T(8,128)(2,1)S(1)} collective-permute-done((bf16[128,2048]{1,0:T(8,128)(2,1)S(1)}, bf16[128,2048]{1,0:T(8,128)(2,1)S(1)}, u32[]{:S(2)}, u32[]{:S(2)}) %collective-permute-start.11) | collective-permute-done | bytes 524320 | tf_op jit(solution)/shard_map/ppermute | solution.py:456
  123.5 5.0 %collective-permute-done.14 = bf16[128,2048]{1,0:T(8,128)(2,1)S(1)} collective-permute-done((bf16[128,2048]{1,0:T(8,128)(2,1)S(1)}, bf16[128,2048]{1,0:T(8,128)(2,1)S(1)}, u32[]{:S(2)}, u32[]{:S(2)}) %collective-permute-start.14) | collective-permute-done | bytes 524320 | tf_op jit(solution)/shard_map/ppermute | solution.py:460
  137.5 6.2 %collective-permute-done.17.refs_1_ = bf16[128,2048]{1,0:T(8,128)(2,1)S(1)} collective-permute-done((bf16[128,2048]{1,0:T(8,128)(2,1)S(1)}, bf16[128,2048]{1,0:T(8,128)(2,1)S(1)}, u32[]{:S(2)}, u32[]{:S(2)}) %collective-permute-start.17) | collective-permute-done | bytes 524320 | tf_op jit(solution)/shard_map/ppermute | solution.py:460
  148.9 6.5 %collective-permute-done.20.refs_8_ = bf16[128,2048]{1,0:T(8,128)(2,1)S(1)} collective-permute-done((bf16[128,2048]{1,0:T(8,128)(2,1)S(1)}, bf16[128,2048]{1,0:T(8,128)(2,1)S(1)}, u32[]{:S(2)}, u32[]{:S(2)}) %collective-permute-start.20) | collective-permute-done | bytes 524320 | tf_op jit(solution)/shard_map/ppermute | solution.py:452
  165.1 27.3 %ffn.1 = (bf16[1024,2048]{1,0:T(8,128)(2,1)}, bf16[704,1024]{1,0:T(8,128)(2,1)}, bf16[2,704,1024]{2,1,0:T(8,128)(2,1)}, bf16[128,2048]{1,0:T(8,128)(2,1)}, bf16[...) custom-call(s32[1]{0:T(128)} %bitcast.8.at, ...), custom_call_target="tpu_custom_call" | custom-call | flops 28000000000 | bytes 84000000 | tf_op jit(solution)/shard_map/ffn/pallas_call | solution.py:576
  199.1 10.3 %ffn_grads.2 = bf16[704,3072]{1,0:T(8,128)(2,1)} custom-call(s32[2]{0:T(128)S(1)} %pad_add_fusion.at, bf16[2,704,1024]{2,1,0:T(8,128)(2,1)S(1)} %copy-done.9, bf16[704,1024]{1,0:T(8,128)(2,1)S(1)} %copy-done.10, bf16[1024,2048]{1,0:T(8,128)(2,1)} %get-tuple-element.305.rows_ref, bf16[1024,2048]{1,0:T(8,128)(2,1)} %all-gather.3.cloned.1.call-done.refs_9_.grad_ref), custom_call_target="tpu_custom_call" | custom-call | flops 8999999488 | bytes 27000000 | tf_op jit(solution)/shard_map/ffn_grads/pallas_call | solution.py:610
  209.4 8.9 %collective-permute-start.30 = (bf16[704,3072]{1,0:T(8,128)(2,1)}, bf16[704,3072]{1,0:T(8,128)(2,1)S(1)}, u32[]{:S(2)}, u32[]{:S(2)}) collective-permute-start(bf16[704,3072]{1,0:T(8,128)(2,1)} %ffn_grads.2), channel_id=1, source_target_pairs={{0,8},{8,0},{1,9},{9,1},{2,10},{10,2},{3,11},{11,3},{4,12},{12,4},... | collective-permute-start | bytes 12976136 | tf_op jit(solution)/shard_map/ppermute | solution.py:810
  222.6 10.2 %collective-permute-done.27 = bf16[128,2048]{1,0:T(8,128)(2,1)S(1)} collective-permute-done((bf16[128,2048]{1,0:T(8,128)(2,1)S(1)}, bf16[128,2048]{1,0:T(8,128)(2,1)S(1)}, u32[]{:S(2)}, u32[]{:S(2)}) %collective-permute-start.27) | collective-permute-done | bytes 524320 | tf_op jit(solution)/shard_map/ppermute | solution.py:456
  241.0 11.0 %ffn_grads.3 = bf16[704,3072]{1,0:T(8,128)(2,1)} custom-call(s32[2]{0:T(128)S(1)} %pad_add_fusion.1.at.where.order, bf16[2,704,1024]{2,1,0:T(8,128)(2,1)S(1)} %copy-done.9, bf16[704,1024]{1,0:T(8,128)(2,1)S(1)} %copy-done.10, bf16[1024,2048]{1,0:T(8,128)(2,1)} %get-tuple-element.305.rows_ref, ...), custom_call_target="tpu_custom_call" | custom-call | flops 8999999488 | bytes 27000000 | tf_op jit(solution)/shard_map/ffn_grads/pallas_call | solution.py:610
  261.2 7.5 %collective-permute-done.34.refs_1_ = bf16[128,2048]{1,0:T(8,128)(2,1)S(1)} collective-permute-done((bf16[128,2048]{1,0:T(8,128)(2,1)S(1)}, bf16[128,2048]{1,0:T(8,128)(2,1)S(1)}, u32[]{:S(2)}, u32[]{:S(2)}) %collective-permute-start.34) | collective-permute-done | bytes 524320 | tf_op jit(solution)/shard_map/ppermute | solution.py:460
  273.6 5.0 %convolution_convert_fusion = bf16[1024,2048]{1,0:T(8,128)(2,1)} fusion(bf16[704,1024]{1,0:T(8,128)(2,1)S(1)} %copy-done.11, bf16[704,2048]{1,0:T(8,128)(2,1)S(1)} %copy-done.57), kind=kOutput, calls=%fused_computation.3 | convolution fusion | flops 2954887168 | bytes 8519680 | tf_op jit(solution)/shard_map/dot_general | solution.py:506
  286.3 5.3 %collective-permute-done.40.refs_5_ = bf16[64,2048]{1,0:T(8,128)(2,1)S(1)} collective-permute-done((bf16[64,2048]{1,0:T(8,128)(2,1)S(1)}, bf16[64,2048]{1,0:T(8,128)(2,1)S(1)}, u32[]{:S(2)}, u32[]{:S(2)}) %collective-permute-start.40) | collective-permute-done | bytes 262176 | tf_op jit(solution)/shard_map/ppermute | solution.py:452
  291.7 10.7 %reduce-scatter.3.cloned.1.call-done = bf16[176,3072]{1,0:T(8,128)(2,1)} async-done(((bf16[704,3072]{1,0:T(8,128)(2,1)}), bf16[176,3072]{1,0:T(8,128)(2,1)}) %reduce-scatter.3.cloned.1.call-update) | async-done | bytes 1081360 | tf_op jit(solution)/shard_map/reduce_scatter | solution.py:811
  305.3 24.4 %mixer_bwd.1 = (bf16[2,512,2048]{2,1,0:T(8,128)(2,1)}, bf16[2,512,1152]{2,1,0:T(8,128)(2,1)}, f32[2,3,4,256]{3,2,1,0:T(4,128)}, f32[2,8,128]{2,1,0:T(8,128)}) custom-call(s32[8]{0:T(128)} %fusion.16.slots, bf16[128,2048]{1,0:T(8,128)(2,1)} %copy-done.25, bf16[128,2048]{1,0:T(8,128)(2,1)} %copy-done.66, bf16[128,2048]{1,0:T(8,128)(2,1)} %copy-done.68, ...), custom_call_target="tpu_custom_call" | custom-call | flops 32000000000 | bytes 96000000 | tf_op jit(solution)/shard_map/mixer_bwd/pallas_call | solution.py:361
  332.8 8.5 %mixer_grads.2 = bf16[4,320,1024]{2,1,0:T(8,128)(2,1)} custom-call(s32[2]{0:T(128)S(1)} %pad_add_fusion.at, bf16[1024,2048]{1,0:T(8,128)(2,1)} %bitcast.90, bf16[1024,1152]{1,0:T(8,128)(2,1)S(1)} %bitcast.84, bf16[1024,256]{1,0:T(8,128)(2,1)S(1)} %bitcast.86, bf16[1024,2048]{1,0:T(8,128)(2,1)} %bitcast.108), custom_call_target="tpu_custom_call" | custom-call | flops 8000000000 | bytes 24000000 | tf_op jit(solution)/shard_map/mixer_grads/pallas_call | solution.py:705
  342.4 10.2 %normed_grad.1 = (bf16[128,2048]{1,0:T(8,128)(2,1)S(1)}, bf16[128,2048]{1,0:T(8,128)(2,1)S(1)}, bf16[128,2048]{1,0:T(8,128)(2,1)S(1)}, bf16[128,2048]{1,0:T(8,12...) custom-call(s32[8]{0:T(128)S(1)} %copy-done.8, ...), custom_call_target="tpu_custom_call" | custom-call | flops 8000000000 | bytes 24000000 | tf_op jit(solution)/shard_map/normed_grad/pallas_call | solution.py:426
  355.7 8.9 %mixer_grads.3 = (bf16[320,1024]{1,0:T(8,128)(2,1)S(1)}, bf16[320,1024]{1,0:T(8,128)(2,1)S(1)}, bf16[160,1024]{1,0:T(8,128)(2,1)}, bf16[160,1024]{1,0:T(8,128)(2,1)}, bf16[320,1024]{1,0:T(8,128)(2,1)S(1)}) custom-call(s32[2]{0:T(128)S(1)} %pad_add_fusion.1.at.where.order, bf16[1024,2048]{1,0:T(8,128)(2,1)} %bitcast.91, bf16[1024,1152]{1,0:T(8,128)(2,1)S(1)} %bitcast.85, ...), custom_call_target="tpu_custom_call" | custom-call | flops 8000000000 | bytes 24000000 | tf_op jit(solution)/shard_map/mixer_grads/pallas_call | solution.py:705
  373.3 14.4 %collective-permute-done.49 = bf16[160,1024]{1,0:T(8,128)(2,1)} collective-permute-done((bf16[160,1024]{1,0:T(8,128)(2,1)}, bf16[160,1024]{1,0:T(8,128)(2,1)}, u32[]{:S(2)}, u32[]{:S(2)}) %collective-permute-start.49) | collective-permute-done | bytes 327712 | tf_op jit(solution)/shard_map/ppermute | solution.py:857
  435.7 4.9 collective-permute-done.56
  449.9 7.2 %place_ffn.1 = (f32[2,704,2048]{2,1,0:T(8,128)}, f32[704,2048]{1,0:T(8,128)}) custom-call(s32[2]{0:T(128)S(1)} %pad_add_fusion.1.at.where.order, bf16[704,3072]{1,0:T(8,128)(2,1)S(1)} %copy-done.2, bf16[704,3072]{1,0:T(8,128)(2,1)S(1)} %collective-permute-done.57.other_ref), custom_call_target="tpu_custom_call" | custom-call | flops 8999999488 | bytes 27000000 | tf_op jit(solution)/shard_map/place_ffn/pallas_call | solution.py:645
  464.6 5.7 %place_rows.3 = (f32[2048,4,256]{2,1,0:T(4,128)}, f32[256,2048]{1,0:T(8,128)}) custom-call(s32[2]{0:T(128)} %copy-done.7, bf16[320,1024]{1,0:T(8,128)(2,1)} %copy-done.24, bf16[320,1024]{1,0:T(8,128)(2,1)} %copy-done.36, bf16[320,1024]{1,0:T(8,128)(2,1)} %copy-done.35, bf16[320,1024]{1,0:T(8,128)(2,1)} %copy-done.59), custom_call_target="tpu_custom_call" | custom-call | flops 5000000000 | bytes 15000000 | tf_op jit(solution)/shard_map/place_rows/pallas_call | solution.py:755
  (394 shorter events, 229.8 us)
Async XLA Ops:
  7.2 110.1 %all-gather.3.cloned.1.call-start = ((), (), s32[]{:S(2)}) async-start(), calls=%async_computation.2 | async-start | bytes 5242880 | tf_op jit(solution)/shard_map/all_gather | solution.py:824
  12.0 15.1 %collective-permute-start.1 = (bf16[128,2048]{1,0:T(8,128)(2,1)S(1)}, bf16[128,2048]{1,0:T(8,128)(2,1)S(1)}, u32[]{:S(2)}, u32[]{:S(2)}) collective-permute-start(bf16[128,2048]{1,0:T(8,128)(2,1)S(1)} %fusion.6.refs_0_), channel_id=1, source_target_pairs={{0,2},{2,4},{4,6},{6,0},{1,3},{3,5},{5,7},{7,1},{8,10},{10,12},{12... | collective-permute-start | bytes 1572872 | tf_op jit(solution)/shard_map/ppermute | solution.py:452
  27.1 15.0 %collective-permute-start.4 = (bf16[128,2048]{1,0:T(8,128)(2,1)}, bf16[128,2048]{1,0:T(8,128)(2,1)}, u32[]{:S(2)}, u32[]{:S(2)}) collective-permute-start(bf16[128,2048]{1,0:T(8,128)(2,1)} %collective-permute-done.2.refs_2_), channel_id=1, source_target_pairs={{0,6},{2,0},{4,2},{6,4},{1,7},{3,1},{5,3},{7,5},{8,14},{10,8},{12,... | collective-permute-start | bytes 1572872 | tf_op jit(solution)/shard_map/ppermute | solution.py:456
  53.4 249.0 %reduce-scatter.3.cloned.1.call-start = ((), (), s32[]{:S(2)}) async-start(), calls=%async_computation.3 | async-start | bytes 5406720 | tf_op jit(solution)/shard_map/reduce_scatter | solution.py:811
  193.4 16.0 %collective-permute-start.25 = (bf16[64,2048]{1,0:T(8,128)(2,1)S(1)}, bf16[64,2048]{1,0:T(8,128)(2,1)S(1)}, u32[]{:S(2)}, u32[]{:S(2)}) collective-permute-start(bf16[64,2048]{1,0:T(8,128)(2,1)S(1)} %get-tuple-element.474), channel_id=1, source_target_pairs={{0,6},{2,0},{4,2},{6,4},{1,7},{3,1},{5,3},{7,5},{8,14},{10,8},{12,... | collective-permute-start | bytes 786440 | tf_op jit(solution)/shard_map/ppermute | solution.py:456
  209.4 26.5 %collective-permute-start.30 = (bf16[704,3072]{1,0:T(8,128)(2,1)}, bf16[704,3072]{1,0:T(8,128)(2,1)S(1)}, u32[]{:S(2)}, u32[]{:S(2)}) collective-permute-start(bf16[704,3072]{1,0:T(8,128)(2,1)} %ffn_grads.2), channel_id=1, source_target_pairs={{0,8},{8,0},{1,9},{9,1},{2,10},{10,2},{3,11},{11,3},{4,12},{12,4},... | collective-permute-start | bytes 12976136 | tf_op jit(solution)/shard_map/ppermute | solution.py:810
  218.4 14.4 %collective-permute-start.27 = (bf16[128,2048]{1,0:T(8,128)(2,1)S(1)}, bf16[128,2048]{1,0:T(8,128)(2,1)S(1)}, u32[]{:S(2)}, u32[]{:S(2)}) collective-permute-start(bf16[128,2048]{1,0:T(8,128)(2,1)S(1)} %add_convert_fusion.12), channel_id=1, source_target_pairs={{0,6},{2,0},{4,2},{6,4},{1,7},{3,1},{5,3},{7,5},{8,14},{10,8},{12,... | collective-permute-start | bytes 1572872 | tf_op jit(solution)/shard_map/ppermute | solution.py:456
  221.4 14.4 %collective-permute-start.28 = (bf16[128,2048]{1,0:T(8,128)(2,1)S(1)}, bf16[128,2048]{1,0:T(8,128)(2,1)S(1)}, u32[]{:S(2)}, u32[]{:S(2)}) collective-permute-start(bf16[128,2048]{1,0:T(8,128)(2,1)S(1)} %copy-done.69), channel_id=1, source_target_pairs={{0,2},{2,4},{4,6},{6,0},{1,3},{3,5},{5,7},{7,1},{8,10},{10,12},{12... | collective-permute-start | bytes 1572872 | tf_op jit(solution)/shard_map/ppermute | solution.py:452
  221.5 14.4 %collective-permute-start.29 = (bf16[128,2048]{1,0:T(8,128)(2,1)S(1)}, bf16[128,2048]{1,0:T(8,128)(2,1)S(1)}, u32[]{:S(2)}, u32[]{:S(2)}) collective-permute-start(bf16[128,2048]{1,0:T(8,128)(2,1)S(1)} %add_convert_fusion.11), channel_id=1, source_target_pairs={{0,1},{1,0},{2,3},{3,2},{4,5},{5,4},{6,7},{7,6},{8,9},{9,8},{10,11... | collective-permute-start | bytes 1572872 | tf_op jit(solution)/shard_map/ppermute | solution.py:460
  253.7 159.5 %all-gather.5.cloned.1.call-start = ((), (), s32[]{:S(2)}) async-start(), calls=%async_computation.4 | async-start | bytes 5406720 | tf_op jit(solution)/shard_map/all_gather | solution.py:858
  302.4 27.4 %collective-permute-start.42 = (bf16[176,3072]{1,0:T(8,128)(2,1)}, bf16[176,3072]{1,0:T(8,128)(2,1)}, u32[]{:S(2)}, u32[]{:S(2)}) collective-permute-start(bf16[176,3072]{1,0:T(8,128)(2,1)} %reduce-scatter.3.cloned.1.call-done), channel_id=1, source_target_pairs={{0,16},{16,0},{1,17},{17,1},{2,18},{18,2},{3,19},{19,3},{4,20},{20... | collective-permute-start | bytes 3244040 | tf_op jit(solution)/shard_map/ppermute | solution.py:778
  342.3 131.0 %reduce-scatter.5.cloned.1.call-start = ((), (), s32[]{:S(2)}) async-start(), calls=%async_computation.5 | async-start | bytes 5242880 | tf_op jit(solution)/shard_map/reduce_scatter | solution.py:877
  366.4 21.4 %collective-permute-start.46 = (bf16[128,2048]{1,0:T(8,128)(2,1)}, bf16[128,2048]{1,0:T(8,128)(2,1)}, u32[]{:S(2)}, u32[]{:S(2)}) collective-permute-start(bf16[128,2048]{1,0:T(8,128)(2,1)} %add_convert_fusion.8), channel_id=1, source_target_pairs={{0,6},{2,0},{4,2},{6,4},{1,7},{3,1},{5,3},{7,5},{8,14},{10,8},{12,... | collective-permute-start | bytes 1572872 | tf_op jit(solution)/shard_map/ppermute | solution.py:456
  369.0 18.8 %collective-permute-start.47 = (bf16[128,2048]{1,0:T(8,128)(2,1)}, bf16[128,2048]{1,0:T(8,128)(2,1)}, u32[]{:S(2)}, u32[]{:S(2)}) collective-permute-start(bf16[128,2048]{1,0:T(8,128)(2,1)} %get-tuple-element.389), channel_id=1, source_target_pairs={{0,2},{2,4},{4,6},{6,0},{1,3},{3,5},{5,7},{7,1},{8,10},{10,12},{12... | collective-permute-start | bytes 1572872 | tf_op jit(solution)/shard_map/ppermute | solution.py:452
  369.0 18.8 %collective-permute-start.48 = (bf16[128,2048]{1,0:T(8,128)(2,1)}, bf16[128,2048]{1,0:T(8,128)(2,1)}, u32[]{:S(2)}, u32[]{:S(2)}) collective-permute-start(bf16[128,2048]{1,0:T(8,128)(2,1)} %add_convert_fusion.7), channel_id=1, source_target_pairs={{0,1},{1,0},{2,3},{3,2},{4,5},{5,4},{6,7},{7,6},{8,9},{9,8},{10,11... | collective-permute-start | bytes 1572872 | tf_op jit(solution)/shard_map/ppermute | solution.py:460
  370.1 17.7 %collective-permute-start.49 = (bf16[160,1024]{1,0:T(8,128)(2,1)}, bf16[160,1024]{1,0:T(8,128)(2,1)}, u32[]{:S(2)}, u32[]{:S(2)}) collective-permute-start(bf16[160,1024]{1,0:T(8,128)(2,1)} %get-tuple-element.393), channel_id=1, source_target_pairs={{0,32},{32,64},{64,96},{96,0},{1,33},{33,65},{65,97},{97,1},{2,34}... | collective-permute-start | bytes 983048 | tf_op jit(solution)/shard_map/ppermute | solution.py:857
  370.1 17.7 %collective-permute-start.50 = (bf16[160,1024]{1,0:T(8,128)(2,1)}, bf16[160,1024]{1,0:T(8,128)(2,1)}, u32[]{:S(2)}, u32[]{:S(2)}) collective-permute-start(bf16[160,1024]{1,0:T(8,128)(2,1)} %get-tuple-element.395), channel_id=1, source_target_pairs={{0,96},{32,0},{64,32},{96,64},{1,97},{33,1},{65,33},{97,65},{2,98}... | collective-permute-start | bytes 983048 | tf_op jit(solution)/shard_map/ppermute | solution.py:857
  389.8 23.4 %collective-permute-start.54 = (bf16[320,1024]{1,0:T(8,128)(2,1)}, bf16[320,1024]{1,0:T(8,128)(2,1)}, u32[]{:S(2)}, u32[]{:S(2)}) collective-permute-start(bf16[320,1024]{1,0:T(8,128)(2,1)} %add_convert_fusion.4), channel_id=1, source_target_pairs={{0,32},{32,64},{64,96},{96,0},{1,33},{33,65},{65,97},{97,1},{2,34}... | collective-permute-start | bytes 1966088 | tf_op jit(solution)/shard_map/ppermute | solution.py:857
  391.8 21.3 %collective-permute-start.55 = (bf16[320,1024]{1,0:T(8,128)(2,1)}, bf16[320,1024]{1,0:T(8,128)(2,1)}, u32[]{:S(2)}, u32[]{:S(2)}) collective-permute-start(bf16[320,1024]{1,0:T(8,128)(2,1)} %add_convert_fusion.3), channel_id=1, source_target_pairs={{0,96},{32,0},{64,32},{96,64},{1,97},{33,1},{65,33},{97,65},{2,98}... | collective-permute-start | bytes 1966088 | tf_op jit(solution)/shard_map/ppermute | solution.py:857
  415.6 25.0 %collective-permute-start.57 = (bf16[704,3072]{1,0:T(8,128)(2,1)}, bf16[704,3072]{1,0:T(8,128)(2,1)S(1)}, u32[]{:S(2)}, u32[]{:S(2)}) collective-permute-start(bf16[704,3072]{1,0:T(8,128)(2,1)} %all-gather.5.cloned.1.call-done.own_ref), channel_id=1, source_target_pairs={{0,8},{8,0},{1,9},{9,1},{2,10},{10,2},{3,11},{11,3},{4,12},{12,4},... | collective-permute-start | bytes 12976136 | tf_op jit(solution)/shard_map/ppermute | solution.py:810
  422.8 17.8 %collective-permute-start.56 = (bf16[320,1024]{1,0:T(8,128)(2,1)S(1)}, bf16[320,1024]{1,0:T(8,128)(2,1)S(1)}, u32[]{:S(2)}, u32[]{:S(2)}) collective-permute-start(bf16[320,1024]{1,0:T(8,128)(2,1)S(1)} %add_convert_fusion.2), channel_id=1, source_target_pairs={{0,16},{16,0},{1,17},{17,1},{2,18},{18,2},{3,19},{19,3},{4,20},{20... | collective-permute-start | bytes 1966088 | tf_op jit(solution)/shard_map/ppermute | solution.py:883
  440.9 16.8 %collective-permute-start.61 = (bf16[320,1024]{1,0:T(8,128)(2,1)S(1)}, bf16[320,1024]{1,0:T(8,128)(2,1)S(1)}, u32[]{:S(2)}, u32[]{:S(2)}) collective-permute-start(bf16[320,1024]{1,0:T(8,128)(2,1)S(1)} %add_convert_fusion.1.refs_0_), channel_id=1, source_target_pairs={{0,32},{32,64},{64,96},{96,0},{1,33},{33,65},{65,97},{97,1},{2,34}... | collective-permute-start | bytes 1966088 | tf_op jit(solution)/shard_map/ppermute | solution.py:857
  441.0 16.7 %collective-permute-start.62 = (bf16[320,1024]{1,0:T(8,128)(2,1)S(1)}, bf16[320,1024]{1,0:T(8,128)(2,1)S(1)}, u32[]{:S(2)}, u32[]{:S(2)}) collective-permute-start(bf16[320,1024]{1,0:T(8,128)(2,1)S(1)} %add_convert_fusion.1.refs_0_), channel_id=1, source_target_pairs={{0,96},{32,0},{64,32},{96,64},{1,97},{33,1},{65,33},{97,65},{2,98}... | collective-permute-start | bytes 1966088 | tf_op jit(solution)/shard_map/ppermute | solution.py:857
  458.6 14.6 %collective-permute-start.67 = (bf16[320,1024]{1,0:T(8,128)(2,1)S(1)}, bf16[320,1024]{1,0:T(8,128)(2,1)S(1)}, u32[]{:S(2)}, u32[]{:S(2)}) collective-permute-start(bf16[320,1024]{1,0:T(8,128)(2,1)S(1)} %collective-permute-done.62.refs_1_), channel_id=1, source_target_pairs={{0,8},{8,0},{1,9},{9,1},{2,10},{10,2},{3,11},{11,3},{4,12},{12,4},... | collective-permute-start | bytes 1966088 | tf_op jit(solution)/shard_map/ppermute | solution.py:810
  (134 other events, 2047.5 us)
Sparse Core Ops, SparseCore 0:
  53.5 57.9 all-gather.2
  253.8 48.5 reduce-scatter.2
  342.4 58.0 all-gather.4
  415.7 47.8 reduce-scatter.4
